TPU v7x, 128 devices: a whole 4x4x4 slice. The times are simulated.
128 devices in a mesh: dp: 16 (over y, z_hi, core), space: 8 (over x, z_lo).
Axes of the slice: x: 4, y: 4, z: 4 (z_hi: 2, z_lo: 2; z = z_hi * 2 + z_lo), core: 2. Of those that a mesh axis runs over, the one named last changes fastest.
Arguments:
- inputs: bfloat16 [128, 32, 32, 1024], P('dp', None, 'space'), may hold values from 0 to 2
- conv_in: bfloat16 [64, 864], replicated, may hold values from -0.21875 to 0.21875
- norm_gain: float32 [64], replicated, may hold values from 0.5 to 1.5
- norm_shift: float32 [64], replicated, may hold values from -3 to 3
- conv_out: bfloat16 [128, 1728], replicated, may hold values from -0.15625 to 0.15625
- dense_in: bfloat16 [65536, 128], replicated, may hold values from -0.0234375 to 0.0234375
- dense_out: bfloat16 [128, 4], replicated, may hold values from -0.5 to 0.5
- targets: float32 [128, 4], P(('dp', 'space')), may hold values from -6 to 6
Outputs:
- grad_conv_in: float32 [64, 864], replicated
- grad_norm: float32 [2, 64], replicated
- grad_conv_out: float32 [128, 1728], replicated
- grad_dense_in: float32 [65536, 128], P(('dp', 'space'))
- grad_dense_out: float32 [128, 4], replicated
- predictions: float32 [128, 4], P(('dp', 'space'))
All inputs are finite; a program needn't handle non-finite values.
Results may differ from a plain program's by a relative error of at most 0.015.
Values may be sent and summed in bfloat16 or wider, within the bound.
A program may use at most 256 MiB of HBM per device.

v0:
```python
import jax
import jax.numpy as jnp
from jax import lax
from jax.sharding import PartitionSpec as P

C_OUT = 128
GRID = 32


norm_epsilon = 1e-05


def extended_2(cells, sides, width):
    for axis, dim in sides:
        count = lax.axis_size(axis)
        ends = count - 1
        head = lax.slice_in_dim(cells, 0, width, axis=dim)
        tail = lax.slice_in_dim(cells, cells.shape[dim] - width, cells.shape[dim], axis=dim)
        cells = jnp.concatenate(
            [
                lax.ppermute(tail, axis, [(i, (i + 1) % count) for i in range(ends)]),
                cells,
                lax.ppermute(head, axis, [((i + 1) % count, i) for i in range(ends)]),
            ],
            axis=dim,
        )
    return cells


def leaky_relu(values):
    return 0.65 * values + 0.35 * values * jnp.tanh(values)


def slope_of(values):
    bent = jnp.tanh(values)
    return 0.65 + 0.35 * (bent + values * (1.0 - bent * bent))


def plane_shift(volume, step_y, step_z, extent):
    plane_len = extent * extent
    offset = step_y * extent + step_z
    margin = extent + 1
    pad_widths = [(0, 0)] * (volume.ndim - 1) + [(margin, margin)]
    padded = jnp.pad(volume, pad_widths)
    shifted = lax.slice_in_dim(
        padded, margin + offset, margin + offset + plane_len, axis=volume.ndim - 1
    )
    column = lax.broadcasted_iota(jnp.int32, (plane_len,), 0) % extent
    inside = ((column + step_z >= 0) & (column + step_z < extent)).astype(volume.dtype)
    return shifted * inside


def columns(slab_ext, planes, extent):
    pieces = []
    for step_x in (-1, 0, 1):
        plane_set = lax.slice_in_dim(slab_ext, 1 + step_x, 1 + step_x + planes, axis=1)
        for step_y in (-1, 0, 1):
            for step_z in (-1, 0, 1):
                pieces.append(plane_shift(plane_set, step_y, step_z, extent))
    stacked = jnp.stack(pieces, 0)
    return stacked.reshape(len(pieces) * slab_ext.shape[0], planes * extent * extent)


def pad_planes(volume, extent):
    shaped = volume.reshape(volume.shape[0], extent, extent * extent)
    return jnp.pad(shaped, ((0, 0), (1, 1), (0, 0)))


def pool_slab(active, planes, extent):
    samples, channels = (active.shape[0], active.shape[1])
    blocks = active.reshape(samples, channels, planes // 2, 2, extent // 2, 2, extent // 2, 2)
    return (blocks.sum(axis=(3, 5, 7)) * 0.125).reshape(samples, channels, -1)


def unpool_slab(gradient, planes, extent):
    samples, channels = (gradient.shape[0], gradient.shape[1])
    blocks = gradient.reshape(samples, channels, planes // 2, 1, extent // 2, 1, extent // 2, 1)
    wide = jnp.broadcast_to(
        blocks, (samples, channels, planes // 2, 2, extent // 2, 2, extent // 2, 2)
    )
    return wide.reshape(samples, channels, planes * extent * extent) * 0.125


def shards(inputs, conv_in, norm_gain, norm_shift, conv_out, dense_in, dense_out, targets):
    half_grid = GRID // 2
    quarter = GRID // 4
    cell_count = inputs.shape[0] * GRID**3
    extended = extended_2(inputs, (("space", 2),), 1)
    planes = extended.shape[2] - 2

    def first_conv(slab_ext):
        return jnp.dot(conv_in, columns(slab_ext, planes, GRID), preferred_element_type=jnp.float32)

    first_out = lax.map(first_conv, extended)
    local_sum = jnp.sum(first_out, axis=(0, 2))
    average = lax.psum(local_sum, "space") / cell_count
    centred = first_out - average[None, :, None]
    variance = lax.psum(jnp.sum(centred * centred, axis=(0, 2)), "space") / cell_count
    inverse = lax.rsqrt(variance + norm_epsilon)
    whitened = centred * inverse[None, :, None]
    normed = norm_gain[None, :, None] * whitened + norm_shift[None, :, None]
    pooled = pool_slab(leaky_relu(normed), planes, GRID).astype(jnp.bfloat16)
    samples_pooled = lax.all_to_all(pooled, "space", split_axis=0, concat_axis=2, tiled=True)

    def second_conv(volume):
        return jnp.dot(
            conv_out,
            columns(pad_planes(volume, half_grid), half_grid, half_grid),
            preferred_element_type=jnp.float32,
        )

    second_out = lax.map(second_conv, samples_pooled)
    local_samples = second_out.shape[0]
    features = (
        pool_slab(leaky_relu(second_out), half_grid, half_grid)
        .reshape(local_samples, -1)
        .astype(jnp.bfloat16)
    )
    hidden_pre = jnp.dot(features, dense_in, preferred_element_type=jnp.float32)
    hidden = leaky_relu(hidden_pre).astype(jnp.bfloat16)
    predictions = jnp.dot(hidden, dense_out, preferred_element_type=jnp.float32)
    misfit = predictions - targets
    grad_out_local = jnp.dot(hidden.astype(jnp.float32).T, misfit, precision=lax.Precision.HIGHEST)
    back_hidden = (
        jnp.dot(misfit, dense_out.astype(jnp.float32).T, precision=lax.Precision.HIGHEST)
        * slope_of(hidden_pre)
    ).astype(jnp.bfloat16)
    grad_dense_in = lax.psum_scatter(
        lax.dot_general(
            features, back_hidden, (((0,), (0,)), ((), ())), preferred_element_type=jnp.float32
        ),
        ("dp", "space"),
        scatter_dimension=0,
        tiled=True,
    )
    back_features = lax.dot_general(
        back_hidden, dense_in, (((1,), (1,)), ((), ())), preferred_element_type=jnp.float32
    )
    back_features = back_features.reshape(local_samples, C_OUT, quarter**3)
    back_second = (unpool_slab(back_features, half_grid, half_grid) * slope_of(second_out)).astype(
        jnp.bfloat16
    )

    def second_back(running, couple):
        volume, gradient = couple
        padded = pad_planes(volume, half_grid)
        patches = columns(padded, half_grid, half_grid)
        running = running + lax.dot_general(
            gradient, patches, (((1,), (1,)), ((), ())), preferred_element_type=jnp.float32
        )
        patch_grad = lax.dot_general(
            conv_out, gradient, (((0,), (0,)), ((), ())), preferred_element_type=jnp.float32
        )
        _, unfold = jax.vjp(
            lambda whole_pad: columns(whole_pad, half_grid, half_grid), padded.astype(jnp.float32)
        )
        volume_grad = unfold(patch_grad)[0][:, 1:-1, :]
        return (running, volume_grad.reshape(volume.shape).astype(jnp.bfloat16))

    grad_conv_out, back_pooled = lax.scan(
        second_back, jnp.zeros(conv_out.shape, jnp.float32), (samples_pooled, back_second)
    )
    back_slab = lax.all_to_all(back_pooled, "space", split_axis=2, concat_axis=0, tiled=True)
    back_active = unpool_slab(back_slab.astype(jnp.float32), planes, GRID) * slope_of(normed)
    sum_grad = jnp.sum(back_active, axis=(0, 2))
    sum_xgrad = jnp.sum(back_active * whitened, axis=(0, 2))
    group_grad, group_xgrad = lax.psum((sum_grad, sum_xgrad), "space")
    back_first = (norm_gain * inverse)[None, :, None] * (
        back_active
        - group_grad[None, :, None] / cell_count
        - whitened * group_xgrad[None, :, None] / cell_count
    )
    back_first = back_first.astype(jnp.bfloat16)

    def first_back(running, couple):
        slab_ext, gradient = couple
        patches = columns(slab_ext, planes, GRID)
        return (
            running
            + lax.dot_general(
                gradient, patches, (((1,), (1,)), ((), ())), preferred_element_type=jnp.float32
            ),
            None,
        )

    grad_conv_in, _ = lax.scan(
        first_back, jnp.zeros(conv_in.shape, jnp.float32), (extended, back_first)
    )
    grad_norm_local = jnp.stack([sum_xgrad, sum_grad])
    summed = lax.psum(
        (grad_conv_in, grad_norm_local, grad_conv_out, grad_out_local), ("dp", "space")
    )
    return (summed[0], summed[1], summed[2], grad_dense_in, summed[3], predictions)


def solution(mesh):
    placed = (P("dp", None, "space", None), P(), P(), P(), P(), P(), P(), P(("dp", "space"), None))
    return jax.shard_map(
        shards,
        mesh=mesh,
        in_specs=placed,
        out_specs=(P(), P(), P(), P(("dp", "space"), None), P(), P(("dp", "space"), None)),
        check_vma=False,
    )
```

profile of v0, /device:TPU:1, one launch (start us, length us, event | category | flops | bytes accessed | tf_op | source)
XLA Modules:
  0.0 1614.8 jit_solution(11225034496510748048)
XLA Ops:
  13.8 5.8 collective-permute-start
  19.6 8.0 collective-permute-done.1
  29.5 10.2 collective-permute-done
  41.7 4.8 pad_maximum_fusion
  46.5 131.2 %while.34 = (s32[]{:T(128)}, f32[8,64,4096]{2,1,0:T(8,128)}, bf16[8,32,6,1024]{3,2,1,0:T(8,128)(2,1)}, bf16[64,864]{1,0:T(8,128)(2,1)}, s32[]{:T(128)}) while((s32[]{:T(128)}, f32[8,64,4096]{2,1,0:T(8,128)}, bf16[8,32,6,1024]{3,2,1,0:T(8,128)(2,1)}, bf16[64,864]{1,0:T(8,128)(2,1)}, s32[]{:T(128)}) %tuple.124), condition=%wide.region_1.2_spmd, body=%wide.region_0.1_spmd.sunk | while | flops 467173376 | bytes 38973516 | solution.py:94
  71.4 4.6 copy.86
  87.7 4.6 copy.86
  104.0 4.6 copy.86
  120.3 4.6 copy.86
  177.7 12.3 copy.39
  194.0 15.3 psum.56
  209.3 8.1 multiply_reduce_fusion.1
  217.4 12.5 psum.57
  229.9 12.9 fusion.38
  242.8 7.7 reduce_sum.56
  258.0 6.9 all-to-all-done
  272.0 5.6 copy.56
  277.7 5.7 fusion.40
  289.9 7.5 convert_convert_fusion
  298.2 78.6 %fusion.140 = f32[1,128,8,8,8]{4,0,3,2,1:T(1,128)} fusion(bf16[128,8,8,8,128]{4,3,2,1,0:T(8,128)(2,1)} %bitcast.529, bf16[128]{0:T(256)(128)(2,1)S(1)} %get-tuple-element.270), kind=kOutput, calls=%fused_computation.309 | convolution fusion | flops 16777216 | bytes 17039616 | tf_op jit(solution)/shard_map/dot_general | solution.py:136
  376.8 8.7 copy.49
  389.6 11.3 convolution_bitcast_fusion.1
  400.9 6.2 fusion.157
  407.1 11.4 fusion.156
  446.1 5.9 bitcast_multiply_fusion.19
  451.9 5.9 bitcast_multiply_fusion.21
  457.9 7.5 fusion.50
  465.4 8.7 fusion.58
  475.6 5.3 copy.45
  481.4 24.4 %reduce.1 = bf16[4096,64]{1,0:T(8,128)(2,1)} reduce(bf16[4096,1,64]{2,1,0:T(2,128)(2,1)} %bitcast.534, bf16[]{:T(256)} %broadcast.801), dimensions={1}, to_apply=%bitcast.376.reduce_sub_computation | reduce | bytes 1048578
  512.5 10.0 fusion.160
  530.1 11.5 fusion.39
  541.6 15.9 all-reduce.39
  557.5 14.0 multiply_convert_fusion
  571.5 9.8 copy.47
  581.3 136.7 %while.35 = (s32[]{:T(128)}, f32[64,864]{1,0:T(8,128)}, bf16[8,64,4096]{2,1,0:T(8,128)(2,1)}, bf16[8,32,6,1024]{3,2,1,0:T(8,128)(2,1)}, s32[]{:T(128)}, /*index=5*/s32[]{:T(128)}) while((s32[]{:T(128)}, f32[64,864]{1,0:T(8,128)}, bf16[8,64,4096]{2,1,0:T(8,128)(2,1)}, bf16[8,32,6,1024]{3,2,1,0:T(8,128)(2,1)}, s32[]{:T(128)}, ...), condition=%wide.region_13.14_spmd.clone, body=%wide.region_12.13_spmd.clone.sunk | while | flops 467283968 | bytes 40546452 | solution.py:186
  589.9 4.6 copy.87
  606.9 4.6 copy.87
  624.0 4.6 copy.87
  641.0 4.6 copy.87
  658.0 4.6 copy.87
  675.0 4.6 copy.87
  692.1 4.6 copy.87
  709.1 4.6 copy.87
  718.1 25.5 %broadcast_multiply_fusion = f32[65536,128]{1,0:T(8,128)} fusion(f32[128]{0:T(128)S(1)} %copy-done.25, f32[65536]{0:T(1024)} %convert.13), kind=kLoop, calls=%fused_computation.102 | loop fusion | flops 8388608 | bytes 33817088 | tf_op jit(solution)/shard_map/dot_general | solution.py:129
  744.4 77.2 %all-reduce.37 = (f32[2,64]{1,0:T(2,128)}, f32[128,4]{0,1:T(4,128)}) all-reduce(f32[2,64]{1,0:T(2,128)S(1)} %pad_maximum_fusion.1, f32[128,4]{0,1:T(4,128)S(1)} %broadcast_multiply_fusion.1), channel_id=1, replica_groups=mesh['dp'=16,'space'=8] {'dp','space'}, use_global_device_ids=true, to_apply=%region_15.16 | all-reduce | flops 640 | bytes 5120 | tf_op jit(solution)/shard_map/psum | solution.py:190
  821.6 57.1 %all-reduce.42.cloned.1.call-done = (f32[64,864]{1,0:T(8,128)}, f32[128,1728]{0,1:T(8,128)}) async-done(((f32[64,864]{1,0:T(8,128)}, f32[128,1728]{0,1:T(8,128)}), (f32[64,864]{1,0:T(8,128)}, f32[128,1728]{0,1:T(8,128)})) %all-reduce.42.cloned.1.call-update) | async-done | bytes 1105936 | tf_op jit(solution)/shard_map/psum | solution.py:190
  878.7 725.0 %reduce-scatter.2.cloned.1.call-done = f32[512,128]{1,0:T(8,128)} async-done(((f32[65536,128]{1,0:T(8,128)}), f32[512,128]{1,0:T(8,128)}) %reduce-scatter.2.cloned.1.call-update) | async-done | bytes 262160 | tf_op jit(solution)/shard_map/reduce_scatter | solution.py:128
  (731 shorter events, 298.1 us)
Async XLA Ops:
  7.2 270.5 %copy-start = (bf16[128,1728]{0,1:T(8,128)(2,1)S(1)}, bf16[128,1728]{0,1:T(8,128)(2,1)}, u32[]{:S(2)}) copy-start(bf16[128,1728]{0,1:T(8,128)(2,1)} %param.16) | copy-start | bytes 1327108
  7.2 34.5 %copy-start.3 = (bf16[8,32,4,1024]{3,2,1,0:T(4,128)(2,1)S(1)}, bf16[8,32,4,1024]{3,2,1,0:T(4,128)(2,1)}, u32[]{:S(2)}) copy-start(bf16[8,32,4,1024]{3,2,1,0:T(4,128)(2,1)} %param.12) | copy-start | bytes 6291460
  11.5 16.1 collective-permute-start.1
  13.8 26.0 %collective-permute-start = (bf16[8,32,1,1024]{3,1,2,0:T(8,128)(2,1)}, bf16[8,32,1,1024]{3,1,2,0:T(8,128)(2,1)}, u32[]{:S(2)}, u32[]{:S(2)}) collective-permute-start(bf16[8,32,1,1024]{3,1,2,0:T(8,128)(2,1)} %copy.52), channel_id=1, source_target_pairs={{0,1},{1,2},{2,3},{3,4},{4,5},{5,6},{6,7},{8,9},{9,10},{10,11},{11... | collective-permute-start | bytes 1572872 | tf_op jit(solution)/shard_map/ppermute | solution.py:21
  209.3 20.6 %copy-start.22 = (f32[64]{0:T(128)S(1)}, f32[64]{0:T(128)}, u32[]{:S(2)}) copy-start(f32[64]{0:T(128)} %param.14) | copy-start | bytes 772
  209.3 20.6 %copy-start.23 = (f32[64]{0:T(128)S(1)}, f32[64]{0:T(128)}, u32[]{:S(2)}) copy-start(f32[64]{0:T(128)} %param.15) | copy-start | bytes 772
  254.5 10.4 all-to-all-start
  277.6 5.7 copy-start.2
  289.9 7.5 copy-start.26
  289.9 7.6 copy-start.27
  297.6 79.2 %copy-start.29 = (f32[1,4]{1,0:T(1,128)}, f32[1,4]{1,0:T(1,128)S(1)}, u32[]{:S(2)}) copy-start(f32[1,4]{1,0:T(1,128)S(1)} %fusion.150) | copy-start | bytes 52
  388.6 1.0 copy-start.6
  418.5 5.3 copy-start.21
  418.5 5.7 copy-start.20
  418.5 6.0 copy-start.19
  419.9 6.0 copy-start.17
  421.5 4.7 copy-start.15
  423.1 3.4 copy-start.18
  423.5 4.4 copy-start.16
  423.8 4.3 copy-start.14
  424.5 6.3 copy-start.13
  425.9 5.2 copy-start.12
  426.5 7.2 copy-start.11
  427.9 6.2 copy-start.10
  428.2 7.2 copy-start.9
  429.5 7.2 copy-start.8
  430.8 7.2 copy-start.7
  509.0 16.4 %all-to-all-start.1 = ((bf16[8,2,16384]{2,1,0:T(2,128)(2,1)}), bf16[8,2,16384]{2,1,0:T(2,128)(2,1)S(1)}, u32[]{:S(2)}, u32[]{:S(2)}) async-start(bf16[8,2,16384]{2,1,0:T(2,128)(2,1)} %reshape.342), calls=%async_computation.1 | async-start | bytes 1048576 | tf_op jit(solution)/shard_map/all_to_all | solution.py:163
  512.5 366.2 %all-reduce.42.cloned.1.call-start = ((), (), s32[]{:S(2)}) async-start(), calls=%async_computation.4 | async-start | bytes 2228224 | tf_op jit(solution)/shard_map/psum | solution.py:190
  581.3 136.7 %copy-start.25 = (f32[128]{0:T(128)S(1)}, f32[128]{0:T(128)}, u32[]{:S(2)}) copy-start(f32[128]{0:T(128)} %get-tuple-element.269) | copy-start | bytes 1540
  589.9 4.7 copy-start.4
  597.8 0.7 copy-start.5
  606.9 4.7 copy-start.4
  614.9 0.7 copy-start.5
  623.9 4.7 copy-start.4
  631.9 0.7 copy-start.5
  641.0 4.7 copy-start.4
  648.9 0.7 copy-start.5
  658.0 4.7 copy-start.4
  666.0 0.7 copy-start.5
  675.0 4.7 copy-start.4
  683.0 0.7 copy-start.5
  692.0 4.7 copy-start.4
  700.0 0.7 copy-start.5
  709.1 4.7 copy-start.4
  717.0 0.7 copy-start.5
  718.0 885.7 %reduce-scatter.2.cloned.1.call-start = ((), (), s32[]{:S(2)}) async-start(), calls=%async_computation.3 | async-start | bytes 33816576 | tf_op jit(solution)/shard_map/reduce_scatter | solution.py:128
  744.3 863.2 %copy-start.1 = (bf16[128,1728]{0,1:T(8,128)(2,1)S(1)}, bf16[128,1728]{0,1:T(8,128)(2,1)}, u32[]{:S(2)}) copy-start(bf16[128,1728]{0,1:T(8,128)(2,1)} %param.16) | copy-start | bytes 1327108
  (3 other events, 2.0 us)
Sparse Core Ops, SparseCore 0:
  718.1 160.5 all-reduce.41
  881.8 721.8 reduce-scatter.1
where the time goes:
time: 1620 us; the launch traced here: 1610 us
  waiting for transfers between devices  807 us (50%)
  other arithmetic  267 us (16%)
  local copies, waits for them, and re-layouts  221 us (14%)
  matrix products  167 us (10%)
  blocking collectives  121 us (7%)
    reduce_scatter x1, waiting for transfers between devices, shards(): lax.psum_scatter(lax.dot_general(features, back_hidden, (((0,), (0,)), ((...  725 us
    while x416, other arithmetic  107 us
    while x48, local copies, waits for them, and re-layouts  79.7 us
    dot_general x1, matrix products, shards(): lax.dot_general(back_hidden, dense_in, (((1,), (1,)), ((), ())), preferre...  78.6 us
    psum x1, blocking collectives, shards(): lax.psum((grad_conv_in, grad_norm_local, grad_conv_out, grad_out_local),...  77.2 us
    psum x1, waiting for transfers between devices, shards(): lax.psum((grad_conv_in, grad_norm_local, grad_conv_out, grad_out_local),...  57.1 us
    unnamed x94, local copies, waits for them, and re-layouts  53.9 us
  transfers between devices with their start and end apart: 6, of which 5 were waited for; matrix products, arithmetic and copies ran while one was open for 3% of the time, Pallas kernels for 0%

commit v1 on v0

v1 whole, which is shorter than its diff:
```python
import functools

import jax
import jax.numpy as jnp
import numpy as np
from jax import lax
from jax.experimental import pallas as pl
from jax.experimental.pallas import tpu as pltpu
from jax.sharding import PartitionSpec as P

MESH = pl.DeviceIdType.MESH
BF = jnp.bfloat16
F32 = jnp.float32
SPACE, DP = 8, 16
GRID, HALF = 32, 16
EPS = 1e-05
VLIM = 56 << 20

VM = pl.BlockSpec(memory_space=pltpu.VMEM)


def leaky(v):
    return v * (0.65 + 0.35 * jnp.tanh(v))


def slope(v):
    t = jnp.tanh(v)
    return 0.65 + 0.35 * (t + v * (1.0 - t * t))


def shift_masks(extent):
    rows = []
    y, z = np.divmod(np.arange(extent * extent), extent)
    for b in (-1, 0, 1):
        for d in (-1, 0, 1):
            rows.append((y + b >= 0) & (y + b < extent) & (z + d >= 0) & (z + d < extent))
    return np.stack(rows).astype(np.float32)


def spread_matrix(extent):
    y, z = np.divmod(np.arange(extent * extent), extent)
    coarse = (y // 2) * (extent // 2) + z // 2
    return (np.arange((extent // 2) ** 2)[:, None] == coarse[None, :]).astype(np.float32) * 0.125


SHIFTS = [(b, d) for b in (-1, 0, 1) for d in (-1, 0, 1)]


def shifted(block, index, extent, mask):
    b, d = SHIFTS[index]
    step = b * extent + d
    if step == 0:
        return block
    cells = extent * extent
    return pltpu.roll(block, (-step) % cells, 1) * mask[index : index + 1, :]


def greet(axis, count):
    me = lax.axis_index(axis)
    barrier = pltpu.get_barrier_semaphore()

    def signal(k, carry):
        pl.semaphore_signal(
            barrier, inc=1, device_id={axis: lax.rem(me + k, count)}, device_id_type=MESH
        )
        return carry

    lax.fori_loop(1, count, signal, 0)


def await_greetings(count):
    pl.semaphore_wait(pltpu.get_barrier_semaphore(), count)


def send_all(axis, count, source, target, send_sem, recv_sem):
    me = lax.axis_index(axis)

    def send(k, carry):
        to = lax.rem(me + k, count)
        pltpu.make_async_remote_copy(
            source(to), target(me), send_sem.at[k], recv_sem.at[k],
            device_id={axis: to}, device_id_type=MESH,
        ).start()
        return carry

    lax.fori_loop(1, count, send, 0)


def wait_all(axis, count, source, target, send_sem, recv_sem):
    me = lax.axis_index(axis)

    def wait(k, carry):
        fro = lax.rem(me + count - k, count)
        pltpu.make_async_remote_copy(
            source(fro), target(fro), send_sem.at[k], recv_sem.at[k],
            device_id={axis: fro}, device_id_type=MESH,
        ).wait()
        return carry

    lax.fori_loop(1, count, wait, 0)


def exchange_kernel(axis, count, x_ref, y_ref, ssem, rsem):
    greet(axis, count)
    me = lax.axis_index(axis)
    await_greetings(count - 1)
    src, dst = (lambda i: x_ref.at[i]), (lambda i: y_ref.at[i])
    send_all(axis, count, src, dst, ssem, rsem)
    y_ref[me] = x_ref[me]
    wait_all(axis, count, src, dst, ssem, rsem)


def exchange(x, axis, count, cid):
    return pl.pallas_call(
        functools.partial(exchange_kernel, axis, count),
        out_shape=jax.ShapeDtypeStruct(x.shape, x.dtype),
        in_specs=[VM],
        out_specs=VM,
        scratch_shapes=[pltpu.SemaphoreType.DMA((count,))] * 2,
        compiler_params=pltpu.CompilerParams(
            collective_id=cid, has_side_effects=True, vmem_limit_bytes=VLIM
        ),
    )(x)


def halo_kernel(v_ref, h_ref, sem):
    me = lax.axis_index("space")
    right, left = lax.rem(me + 1, SPACE), lax.rem(me + SPACE - 1, SPACE)
    barrier = pltpu.get_barrier_semaphore()
    for other in (left, right):
        pl.semaphore_signal(barrier, inc=1, device_id={"space": other}, device_id_type=MESH)
    pl.semaphore_wait(barrier, 2)
    up = pltpu.make_async_remote_copy(
        v_ref.at[3], h_ref.at[0], sem.at[0], sem.at[1],
        device_id={"space": right}, device_id_type=MESH,
    )
    down = pltpu.make_async_remote_copy(
        v_ref.at[0], h_ref.at[1], sem.at[2], sem.at[3],
        device_id={"space": left}, device_id_type=MESH,
    )
    up.start()
    down.start()
    up.wait()
    down.wait()

    @pl.when(me == 0)
    def _():
        h_ref[0] = jnp.zeros(h_ref.shape[1:], BF)

    @pl.when(me == SPACE - 1)
    def _():
        h_ref[1] = jnp.zeros(h_ref.shape[1:], BF)


def halo(v):
    return pl.pallas_call(
        halo_kernel,
        out_shape=jax.ShapeDtypeStruct((2, 8, 32, 1024), BF),
        in_specs=[VM],
        out_specs=VM,
        scratch_shapes=[pltpu.SemaphoreType.DMA((4,))],
        compiler_params=pltpu.CompilerParams(
            collective_id=1, has_side_effects=True, vmem_limit_bytes=VLIM
        ),
    )(v)


def fill_first(v_ref, h_ref, mask, s_ref):
    block = jnp.concatenate(
        [h_ref[0, 0]] + [v_ref[q, 0] for q in range(4)] + [h_ref[1, 0]], axis=0
    )
    for i in range(9):
        s_ref[i * 192 : (i + 1) * 192, :] = shifted(block, i, GRID, mask)


def first_kernel(v_ref, h_ref, w_ref, m_ref, o_ref, st_ref, s_ref):
    fill_first(v_ref, h_ref, m_ref[...], s_ref)
    out = jnp.dot(w_ref[...], s_ref[...], preferred_element_type=F32)
    o_ref[0] = out
    total = jnp.sum(out, axis=1, keepdims=True)
    off = out - total * (1.0 / 1024)
    spread = jnp.sum(off * off, axis=1, keepdims=True)
    lane = lax.broadcasted_iota(jnp.int32, (256, 128), 1)
    st_ref[0] = jnp.where(lane == 0, total, jnp.where(lane == 1, spread, 0.0))


V_SPEC = pl.BlockSpec((4, 1, 32, 1024), lambda i: (0, i, 0, 0))
H_SPEC = pl.BlockSpec((2, 1, 32, 1024), lambda i: (0, i, 0, 0))


def whole(*shape):
    return pl.BlockSpec(shape, lambda i: (0,) * len(shape))


def by_sample(*shape):
    return pl.BlockSpec((1,) + shape, lambda i: (i,) + (0,) * len(shape))


def first_conv(v, h, w_big, masks):
    return pl.pallas_call(
        first_kernel,
        grid=(8,),
        out_shape=[
            jax.ShapeDtypeStruct((8, 256, 1024), F32),
            jax.ShapeDtypeStruct((8, 256, 128), F32),
        ],
        in_specs=[V_SPEC, H_SPEC, whole(256, 1728), whole(9, 1024)],
        out_specs=[by_sample(256, 1024), by_sample(256, 128)],
        scratch_shapes=[pltpu.VMEM((1728, 1024), BF)],
        compiler_params=pltpu.CompilerParams(vmem_limit_bytes=VLIM),
    )(v, h, w_big, masks)


def stats_kernel(st_ref, o_ref, send, recv, ssem, rsem):
    greet("space", SPACE)
    me = lax.axis_index("space")
    lane = lax.broadcasted_iota(jnp.int32, (64, 128), 1)
    blocks = [st_ref[i, p * 64 : (p + 1) * 64, :] for i in range(8) for p in range(4)]
    total = functools.reduce(lambda a, b: a + b, blocks)
    mean = total[:, 0:1] * (1.0 / 32768)
    moved = 0.0
    for block in blocks:
        gap = block[:, 0:1] * (1.0 / 1024) - mean
        moved = moved + gap * gap
    spread = total[:, 1:2] + 1024.0 * moved
    send[...] = jnp.where(lane == 0, mean, jnp.where(lane == 1, spread, 0.0))
    recv[me] = send[...]
    await_greetings(SPACE - 1)
    src, dst = (lambda i: send), (lambda i: recv.at[i])
    send_all("space", SPACE, src, dst, ssem, rsem)
    wait_all("space", SPACE, src, dst, ssem, rsem)
    parts = [recv[i] for i in range(8)]
    mean = functools.reduce(lambda a, b: a + b, parts)[:, 0:1] * 0.125
    spread = 0.0
    for part in parts:
        gap = part[:, 0:1] - mean
        spread = spread + part[:, 1:2] + 32768.0 * gap * gap
    inverse = lax.rsqrt(spread * (1.0 / 262144) + EPS)
    tile = jnp.where(lane == 0, mean, jnp.where(lane == 1, inverse, 0.0))
    for p in range(4):
        o_ref[p * 64 : (p + 1) * 64, :] = tile


def stats(st):
    return pl.pallas_call(
        stats_kernel,
        out_shape=jax.ShapeDtypeStruct((256, 128), F32),
        in_specs=[VM],
        out_specs=VM,
        scratch_shapes=[
            pltpu.VMEM((64, 128), F32),
            pltpu.VMEM((8, 64, 128), F32),
            pltpu.SemaphoreType.DMA((8,)),
            pltpu.SemaphoreType.DMA((8,)),
        ],
        compiler_params=pltpu.CompilerParams(collective_id=2, has_side_effects=True),
    )(st)


def pool_kernel(x_ref, st_ref, gs_ref, sp_ref, o_ref):
    white = (x_ref[0] - st_ref[:, 0:1]) * st_ref[:, 1:2]
    act = leaky(gs_ref[:, 0:1] * white + gs_ref[:, 1:2])
    pairs = jnp.concatenate(
        [act[0:64] + act[64:128], act[128:192] + act[192:256]], axis=0
    ).astype(BF)
    o_ref[0] = lax.dot_general(
        pairs, sp_ref[...], (((1,), (1,)), ((), ())), preferred_element_type=F32
    ).astype(BF)


def pool_first(x, st, gs, sp):
    return pl.pallas_call(
        pool_kernel,
        grid=(8,),
        out_shape=jax.ShapeDtypeStruct((8, 128, 256), BF),
        in_specs=[by_sample(256, 1024), whole(256, 128), whole(256, 128), whole(256, 1024)],
        out_specs=by_sample(128, 256),
        compiler_params=pltpu.CompilerParams(vmem_limit_bytes=VLIM),
    )(x, st, gs, sp)


def fill_second(p_ref, mask, s_ref):
    s_ref[0] = jnp.zeros((576, 256), BF)
    s_ref[17] = jnp.zeros((576, 256), BF)
    block = p_ref[...]
    for i in range(9):
        s_ref[1:17, i * 64 : (i + 1) * 64, :] = shifted(block, i, HALF, mask).reshape(16, 64, 256)


def second_kernel(p_ref, w_ref, m_ref, sp_ref, o_ref, f_ref, s_ref):
    fill_second(p_ref, m_ref[...], s_ref)
    for k in range(8):
        act = 0.0
        for p in (2 * k, 2 * k + 1):
            out = jnp.dot(
                w_ref[...], s_ref[p : p + 3].reshape(1728, 256), preferred_element_type=F32
            )
            o_ref[p] = out
            act = act + leaky(out)
        f_ref[:, k * 64 : (k + 1) * 64] = lax.dot_general(
            act.astype(BF), sp_ref[...], (((1,), (1,)), ((), ())), preferred_element_type=F32
        ).astype(BF)


def second_conv(pooled, w, masks, sp):
    return pl.pallas_call(
        second_kernel,
        out_shape=[
            jax.ShapeDtypeStruct((16, 128, 256), F32),
            jax.ShapeDtypeStruct((128, 512), BF),
        ],
        in_specs=[VM] * 4,
        out_specs=[VM] * 2,
        scratch_shapes=[pltpu.VMEM((18, 576, 256), BF)],
        compiler_params=pltpu.CompilerParams(vmem_limit_bytes=VLIM),
    )(pooled, w, masks, sp)


def dense_kernel(
    f_ref, d_ref, do_ref, tg_ref,
    b_ref, fx_ref, bh_ref, small_ref,
    dv, part, got, bsend, q_send, ssem, rsem, dsem,
):
    greet("space", SPACE)
    me = lax.axis_index("space")

    def fetch(d):
        return pltpu.make_async_copy(d_ref.at[d, me], dv.at[d], dsem.at[d])

    for d in range(16):
        fetch(d).start()
    await_greetings(SPACE - 1)

    src, dst = (lambda i: f_ref.at[i]), (lambda i: fx_ref.at[i])
    send_all("space", SPACE, src, dst, ssem.at[0], rsem.at[0])
    fx_ref[me] = f_ref[me]
    for d in range(16):
        fetch(d).wait()
    wait_all("space", SPACE, src, dst, ssem.at[0], rsem.at[0])

    feats = fx_ref[...].reshape(128, 512)
    row = lax.broadcasted_iota(jnp.int32, (128, 128), 0) % 16
    total = jnp.zeros((128, 128), F32)
    for d in range(16):
        product = jnp.dot(feats, dv[d], preferred_element_type=F32)
        total = total + jnp.where(row == d, product, 0.0)
    total = total.reshape(8, 16, 128)
    part[...] = total[:, 0:8] + total[:, 8:16]
    src, dst = (lambda i: part.at[i]), (lambda i: got.at[i])
    send_all("space", SPACE, src, dst, ssem.at[1], rsem.at[1])
    got[me] = part[me]
    wait_all("space", SPACE, src, dst, ssem.at[1], rsem.at[1])

    hidden_pre = jnp.sum(jnp.sum(got[...], axis=0), axis=0, keepdims=True)
    hidden = leaky(hidden_pre).astype(BF).astype(F32)
    out_t = do_ref[...]
    predictions = jnp.sum(hidden * out_t, axis=1, keepdims=True)
    misfit = predictions - tg_ref[:, 0:1]
    small_ref[0] = hidden * misfit
    small_ref[1] = jnp.broadcast_to(predictions, (8, 128))
    back = jnp.sum(misfit * out_t, axis=0, keepdims=True) * slope(hidden_pre)
    bsend[...] = jnp.broadcast_to(back, (16, 128)).astype(BF)
    src, dst = (lambda i: bsend), (lambda i: bh_ref.at[i])
    send_all("space", SPACE, src, dst, ssem.at[2], rsem.at[2])
    bh_ref[me] = bsend[...]
    wait_all("space", SPACE, src, dst, ssem.at[2], rsem.at[2])

    backs = bh_ref[...].reshape(128, 128)
    row = lax.broadcasted_iota(jnp.int32, (128, 512), 0) % 16
    total = jnp.zeros((128, 512), F32)
    for d in range(16):
        product = lax.dot_general(
            backs, dv[d], (((1,), (1,)), ((), ())), preferred_element_type=F32
        )
        total = jnp.where(row == d, product, total)
    q_send[...] = total.astype(BF).reshape(8, 16, 512)
    src, dst = (lambda i: q_send.at[i]), (lambda i: b_ref.at[i])
    send_all("space", SPACE, src, dst, ssem.at[3], rsem.at[3])
    b_ref[me] = q_send[me]
    wait_all("space", SPACE, src, dst, ssem.at[3], rsem.at[3])


def dense(feats, dense_in, out_t, tg):
    return pl.pallas_call(
        dense_kernel,
        out_shape=[
            jax.ShapeDtypeStruct((8, 16, 512), BF),
            jax.ShapeDtypeStruct((8, 16, 512), BF),
            jax.ShapeDtypeStruct((8, 16, 128), BF),
            jax.ShapeDtypeStruct((2, 8, 128), F32),
        ],
        in_specs=[VM, pl.BlockSpec(memory_space=pl.ANY), VM, VM],
        out_specs=[VM] * 4,
        scratch_shapes=[
            pltpu.VMEM((16, 512, 128), BF),
            pltpu.VMEM((8, 8, 128), F32),
            pltpu.VMEM((8, 8, 128), F32),
            pltpu.VMEM((16, 128), BF),
            pltpu.VMEM((8, 16, 512), BF),
            pltpu.SemaphoreType.DMA((4, 8)),
            pltpu.SemaphoreType.DMA((4, 8)),
            pltpu.SemaphoreType.DMA((16,)),
        ],
        compiler_params=pltpu.CompilerParams(
            collective_id=3, has_side_effects=True, vmem_limit_bytes=VLIM
        ),
    )(feats, dense_in, out_t, tg)


def second_back_kernel(p_ref, x_ref, b_ref, w_ref, m_ref, sp_ref, o_ref, gw_ref, s_ref, g_ref):
    masks = m_ref[...]
    fill_second(p_ref, masks, s_ref)
    g_ref[0] = jnp.zeros((128, 256), BF)
    g_ref[17] = jnp.zeros((128, 256), BF)
    for k in range(8):
        wide = jnp.dot(
            b_ref[:, k * 64 : (k + 1) * 64], sp_ref[...], preferred_element_type=F32
        )
        for p in (2 * k, 2 * k + 1):
            g_ref[p + 1] = (wide * slope(x_ref[p])).astype(BF)
    gw_ref[...] = jnp.zeros((128, 1728), F32)

    def plane(p, carry):
        gw_ref[...] += lax.dot_general(
            g_ref[p + 1],
            s_ref[pl.ds(p, 3)].reshape(1728, 256),
            (((1,), (1,)), ((), ())),
            preferred_element_type=F32,
        )
        taps = jnp.dot(
            w_ref[...], g_ref[pl.ds(p, 3)].reshape(384, 256), preferred_element_type=F32
        )
        total = taps[256:320]
        for i in range(9):
            if i != 4:
                total = total + shifted(
                    taps[i * 64 : (i + 1) * 64], 8 - i, HALF, masks.astype(F32)
                )
        o_ref[p] = total.astype(BF)
        return carry

    lax.fori_loop(0, 16, plane, 0)


def second_back(pooled, x, b, w_back, masks, sp):
    return pl.pallas_call(
        second_back_kernel,
        out_shape=[
            jax.ShapeDtypeStruct((16, 64, 256), BF),
            jax.ShapeDtypeStruct((128, 1728), F32),
        ],
        in_specs=[VM] * 6,
        out_specs=[VM] * 2,
        scratch_shapes=[pltpu.VMEM((18, 576, 256), BF), pltpu.VMEM((18, 128, 256), BF)],
        compiler_params=pltpu.CompilerParams(vmem_limit_bytes=VLIM),
    )(pooled, x, b, w_back, masks, sp)


def active_kernel(x_ref, b_ref, st_ref, gs_ref, sp_ref, o_ref, sum_ref):
    white = (x_ref[0] - st_ref[:, 0:1]) * st_ref[:, 1:2]
    bent = slope(gs_ref[:, 0:1] * white + gs_ref[:, 1:2])
    wide = jnp.dot(b_ref[0], sp_ref[...], preferred_element_type=F32)
    wide = jnp.concatenate([wide[0:64], wide[0:64], wide[64:128], wide[64:128]], axis=0)
    active = wide * bent
    o_ref[0] = active.astype(BF)
    lane = lax.broadcasted_iota(jnp.int32, (256, 128), 1)
    grad = jnp.sum(active, axis=1, keepdims=True)
    xgrad = jnp.sum(active * white, axis=1, keepdims=True)
    tile = jnp.where(lane == 0, grad, jnp.where(lane == 1, xgrad, 0.0))

    @pl.when(pl.program_id(0) == 0)
    def _():
        sum_ref[...] = tile

    @pl.when(pl.program_id(0) > 0)
    def _():
        sum_ref[...] += tile


def back_active(x, b, st, gs, sp):
    return pl.pallas_call(
        active_kernel,
        grid=(8,),
        out_shape=[
            jax.ShapeDtypeStruct((8, 256, 1024), BF),
            jax.ShapeDtypeStruct((256, 128), F32),
        ],
        in_specs=[
            by_sample(256, 1024), by_sample(128, 256),
            whole(256, 128), whole(256, 128), whole(256, 1024),
        ],
        out_specs=[by_sample(256, 1024), whole(256, 128)],
        compiler_params=pltpu.CompilerParams(vmem_limit_bytes=VLIM),
    )(x, b, st, gs, sp)


def sums_kernel(s_ref, o_ref, own_ref, recv, ssem, rsem):
    greet("space", SPACE)
    me = lax.axis_index("space")
    own_ref[...] = (
        s_ref[0:64, :] + s_ref[64:128, :] + s_ref[128:192, :] + s_ref[192:256, :]
    )
    recv[me] = own_ref[...]
    await_greetings(SPACE - 1)
    src, dst = (lambda i: own_ref), (lambda i: recv.at[i])
    send_all("space", SPACE, src, dst, ssem, rsem)
    wait_all("space", SPACE, src, dst, ssem, rsem)
    tile = jnp.sum(recv[...], axis=0) * (1.0 / 262144)
    for p in range(4):
        o_ref[p * 64 : (p + 1) * 64, :] = tile


def group_sums(s):
    return pl.pallas_call(
        sums_kernel,
        out_shape=[jax.ShapeDtypeStruct((256, 128), F32), jax.ShapeDtypeStruct((64, 128), F32)],
        in_specs=[VM],
        out_specs=[VM] * 2,
        scratch_shapes=[
            pltpu.VMEM((8, 64, 128), F32),
            pltpu.SemaphoreType.DMA((8,)),
            pltpu.SemaphoreType.DMA((8,)),
        ],
        compiler_params=pltpu.CompilerParams(collective_id=4, has_side_effects=True),
    )(s)


def first_back_kernel(
    x_ref, a_ref, v_ref, h_ref, st_ref, gs_ref, gh_ref, m_ref, o_ref, s_ref, acc
):
    fill_first(v_ref, h_ref, m_ref[...], s_ref)
    white = (x_ref[0] - st_ref[:, 0:1]) * st_ref[:, 1:2]
    back = (gs_ref[:, 0:1] * st_ref[:, 1:2]) * (
        a_ref[0].astype(F32) - gh_ref[:, 0:1] - white * gh_ref[:, 1:2]
    )
    product = lax.dot_general(
        back.astype(BF), s_ref[...], (((1,), (1,)), ((), ())), preferred_element_type=F32
    )

    @pl.when(pl.program_id(0) == 0)
    def _():
        acc[...] = product

    @pl.when(pl.program_id(0) > 0)
    def _():
        acc[...] += product

    @pl.when(pl.program_id(0) == 7)
    def _():
        for i in range(9):
            for a in range(3):
                total = 0.0
                for p in range(4):
                    at = i * 192 + (p + a) * 32
                    total = total + acc[p * 64 : (p + 1) * 64, at : at + 32]
                o_ref[:, (a * 9 + i) * 32 : (a * 9 + i + 1) * 32] = total


def first_back(x, a, v, h, st, gs, gh, masks):
    return pl.pallas_call(
        first_back_kernel,
        grid=(8,),
        out_shape=jax.ShapeDtypeStruct((64, 864), F32),
        in_specs=[
            by_sample(256, 1024), by_sample(256, 1024), V_SPEC, H_SPEC,
            whole(256, 128), whole(256, 128), whole(256, 128), whole(9, 1024),
        ],
        out_specs=whole(64, 864),
        scratch_shapes=[pltpu.VMEM((1728, 1024), BF), pltpu.VMEM((256, 1728), F32)],
        compiler_params=pltpu.CompilerParams(vmem_limit_bytes=VLIM),
    )(x, a, v, h, st, gs, gh, masks)


LANES = 2176
TILES = LANES // 128


def reduce_kernel(
    x_ref, fx_ref, bh_ref,
    o_ref, f_ref, ba_ref,
    got1, tiles, got2, piece, got3, strip, ssem, rsem, tsem, usem,
):
    greet("space", SPACE)
    greet("dp", DP)
    me, group = lax.axis_index("space"), lax.axis_index("dp")
    await_greetings(SPACE - 1 + DP - 1)

    src1, dst1 = (lambda i: x_ref.at[i]), (lambda i: got1.at[i])
    send_all("space", SPACE, src1, dst1, ssem.at[0], rsem.at[0])
    src_f, dst_f = (lambda i: fx_ref.at[i]), (lambda i: f_ref.at[i])
    send_all("dp", DP, src_f, dst_f, tsem.at[0], usem.at[0])
    src_b, dst_b = (lambda i: bh_ref), (lambda i: ba_ref.at[i])
    send_all("dp", DP, src_b, dst_b, tsem.at[1], usem.at[1])
    f_ref[group] = fx_ref[group]
    ba_ref[group] = bh_ref[...]
    got1[me] = x_ref[me]
    tiles[TILES:32] = jnp.zeros((32 - TILES, 16, 128), F32)
    wait_all("space", SPACE, src1, dst1, ssem.at[0], rsem.at[0])
    for t in range(TILES):
        tiles[t] = jnp.sum(got1[:, :, t * 128 : (t + 1) * 128], axis=0)

    src2, dst2 = (lambda i: tiles.at[pl.ds(i * 2, 2)]), (lambda i: got2.at[i])
    send_all("dp", DP, src2, dst2, tsem.at[2], usem.at[2])
    got2[group] = tiles[pl.ds(group * 2, 2)]
    wait_all("dp", DP, src2, dst2, tsem.at[2], usem.at[2])
    piece[...] = jnp.sum(got2[...], axis=0)

    src3, dst3 = (lambda i: piece), (lambda i: got3.at[pl.ds(i * 2, 2)])
    send_all("dp", DP, src3, dst3, tsem.at[3], usem.at[3])
    got3[pl.ds(group * 2, 2)] = piece[...]
    wait_all("dp", DP, src3, dst3, tsem.at[3], usem.at[3])
    for t in range(TILES):
        strip[:, t * 128 : (t + 1) * 128] = got3[t]

    src4, dst4 = (lambda i: strip), (lambda i: o_ref.at[i])
    send_all("space", SPACE, src4, dst4, ssem.at[1], rsem.at[1])
    o_ref[me] = strip[...]
    wait_all("space", SPACE, src4, dst4, ssem.at[1], rsem.at[1])
    wait_all("dp", DP, src_f, dst_f, tsem.at[0], usem.at[0])
    wait_all("dp", DP, src_b, dst_b, tsem.at[1], usem.at[1])


def reduce_all(x, fx, bh):
    return pl.pallas_call(
        reduce_kernel,
        out_shape=[
            jax.ShapeDtypeStruct((8, 16, LANES), F32),
            jax.ShapeDtypeStruct((16, 32, 128), BF),
            jax.ShapeDtypeStruct((16, 16, 128), BF),
        ],
        in_specs=[VM] * 3,
        out_specs=[VM] * 3,
        scratch_shapes=[
            pltpu.VMEM((8, 16, LANES), F32),
            pltpu.VMEM((32, 16, 128), F32),
            pltpu.VMEM((16, 2, 16, 128), F32),
            pltpu.VMEM((2, 16, 128), F32),
            pltpu.VMEM((32, 16, 128), F32),
            pltpu.VMEM((16, LANES), F32),
            pltpu.SemaphoreType.DMA((2, 8)),
            pltpu.SemaphoreType.DMA((2, 8)),
            pltpu.SemaphoreType.DMA((4, 16)),
            pltpu.SemaphoreType.DMA((4, 16)),
        ],
        compiler_params=pltpu.CompilerParams(
            collective_id=5, has_side_effects=True, vmem_limit_bytes=VLIM
        ),
    )(x, fx, bh)


def columns_of(first, second):
    tile = jnp.stack([first, second], axis=1)
    return jnp.pad(jnp.tile(tile, (4, 1)), ((0, 0), (0, 126)))


def shards(inputs, conv_in, norm_gain, norm_shift, conv_out, dense_in, dense_out, targets):
    masks1 = jnp.asarray(shift_masks(GRID), BF)
    masks2 = jnp.asarray(shift_masks(HALF), BF)
    spread1 = jnp.asarray(spread_matrix(GRID), BF)
    spread2 = jnp.asarray(spread_matrix(HALF), BF)

    taps = conv_in.reshape(64, 3, 9, 32).transpose(0, 2, 1, 3)
    w_big = jnp.stack(
        [jnp.pad(taps, ((0, 0), (0, 0), (p, 3 - p), (0, 0))) for p in range(4)], axis=0
    ).reshape(256, 1728)
    gs = columns_of(norm_gain, norm_shift)
    w_out = conv_out.reshape(16, 8, 1728).transpose(1, 0, 2).reshape(128, 1728)
    w_back = w_out.reshape(128, 3, 9, 64)[:, ::-1].transpose(2, 3, 1, 0).reshape(576, 384)
    out_t = jnp.pad(dense_out.astype(F32).T, ((0, 4), (0, 0)))
    tg = jnp.broadcast_to(jnp.pad(targets, ((0, 0), (0, 4))).T, (8, 128))

    v = inputs.transpose(2, 0, 1, 3)
    h = halo(v)
    first_out, blocks = first_conv(v, h, w_big, masks1)
    st = stats(blocks)
    pooled = exchange(pool_first(first_out, st, gs, spread1), "space", SPACE, 6)
    pooled = pooled.reshape(1024, 256)
    second_out, feats = second_conv(pooled, w_out, masks2, spread2)
    b_feats, fx, bh, small = dense(
        feats.reshape(8, 16, 512), dense_in.reshape(16, 8, 512, 128), out_t, tg
    )
    back, grad_out = second_back(
        pooled, second_out, b_feats.reshape(128, 512), w_back, masks2, spread2
    )
    back = exchange(back.reshape(8, 128, 256), "space", SPACE, 7)
    active, sums = back_active(first_out, back, st, gs, spread1)
    gh, own = group_sums(sums)
    grad_in = first_back(first_out, active, v, h, st, gs, gh, masks1)

    packed = jnp.concatenate(
        [
            grad_out,
            jnp.concatenate([grad_in[:, :432], grad_in[:, 432:]], axis=0),
            small[0, :4].T,
            jnp.concatenate([own[:, 1:2], own[:, 0:1]], axis=0),
            jnp.zeros((128, LANES - 2165), F32),
        ],
        axis=1,
    )
    fx = fx.transpose(1, 0, 2).reshape(16, 32, 128)
    bh = jnp.pad(bh[:, 0, :], ((0, 8), (0, 0)))
    summed, f_all, bh_all = reduce_all(packed.reshape(8, 16, LANES), fx, bh)
    summed = summed.reshape(128, LANES)
    grad_conv_out = (
        summed[:, :1728].reshape(8, 16, 1728).transpose(1, 0, 2).reshape(128, 1728)
    )
    grad_conv_in = jnp.concatenate([summed[:64, 1728:2160], summed[64:, 1728:2160]], axis=1)
    grad_dense_out = summed[:, 2160:2164]
    grad_norm = summed[:, 2164].reshape(2, 64)
    grad_dense_in = lax.dot_general(
        f_all.reshape(128, 512),
        bh_all[:, :8].reshape(128, 128),
        (((0,), (0,)), ((), ())),
        preferred_element_type=F32,
    )
    predictions = small[1, :4, 0].reshape(1, 4)
    return grad_conv_in, grad_norm, grad_conv_out, grad_dense_in, grad_dense_out, predictions


def solution(mesh):
    placed = (P("dp", None, "space", None), P(), P(), P(), P(), P(), P(), P(("dp", "space"), None))
    return jax.shard_map(
        shards,
        mesh=mesh,
        in_specs=placed,
        out_specs=(P(), P(), P(), P(("dp", "space"), None), P(), P(("dp", "space"), None)),
        check_vma=False,
    )
```

time: 1620 us -> 264 us (0.16)
  waiting for transfers between devices: 807 us -> 0 us
  other arithmetic: 267 us -> 3.23 us
  Pallas kernels: 0 us -> 226 us
  local copies, waits for them, and re-layouts: 221 us -> 28.8 us
  matrix products: 167 us -> 1.67 us
  blocking collectives: 121 us -> 0 us
    reduce_scatter x1 -> x0, waiting for transfers between devices: 725 us -> none  [shards(): lax.psum_scatter(lax.dot_general(features, back_hidden, (((0,), (0,)), ((...]
    pallas_call x0 -> x13, Pallas kernels: none -> 226 us  [the longest x1 66.4 us: reduce_all(): pl.pallas_call(reduce_kernel, out_shape=[jax.ShapeDtypeStruct((8, 16, LAN...]
    dot_general x23 -> x1, matrix products: 167 us -> 1.67 us  [shards(): lax.dot_general(f_all.reshape(128, 512), bh_all[:, :8].reshape(128, 128),...]
    psum x4 -> x0, blocking collectives: 121 us -> none  [the longest x1 77.2 us: shards(): lax.psum((grad_conv_in, grad_norm_local, grad_conv_out, grad_out_local),...]
    while x416 -> x0, other arithmetic: 107 us -> none
    while x49 -> x0, local copies, waits for them, and re-layouts: 92 us -> none
    psum x1 -> x0, waiting for transfers between devices: 57.1 us -> none  [shards(): lax.psum((grad_conv_in, grad_norm_local, grad_conv_out, grad_out_local),...]
    unnamed x94 -> x20, local copies, waits for them, and re-layouts: 53.9 us -> 8.57 us
  transfers between devices with their start and end apart: 6 -> 0, of which waited for: 5 -> 0; matrix products, arithmetic and copies ran while one was open for 3% -> 0% of each run, Pallas kernels for 0% -> 0%
where the time goes in v1:
time: 264 us; the launch traced here: 261 us
  Pallas kernels  226 us (86%)
  local copies, waits for them, and re-layouts  28.8 us (11%)
  other arithmetic  3.23 us (1%)
    pallas_call x1, Pallas kernels, reduce_all(): pl.pallas_call(reduce_kernel, out_shape=[jax.ShapeDtypeStruct((8, 16, LAN...  66.4 us
    pallas_call x1, Pallas kernels, halo(): pl.pallas_call(halo_kernel, out_shape=jax.ShapeDtypeStruct((2, 8, 32, 102...  29.1 us
    pallas_call x1, Pallas kernels, dense(): pl.pallas_call(dense_kernel, out_shape=[jax.ShapeDtypeStruct((8, 16, 512)...  20.3 us
    pallas_call x1, Pallas kernels, first_back(): pl.pallas_call(first_back_kernel, grid=(8,), out_shape=jax.ShapeDtypeStru...  19.5 us
    pallas_call x2, Pallas kernels, exchange(): pl.pallas_call(functools.partial(exchange_kernel, axis, count), out_shape...  18.3 us
    pallas_call x1, Pallas kernels, second_back(): pl.pallas_call(second_back_kernel, out_shape=[jax.ShapeDtypeStruct((16, 6...  15.6 us
    pallas_call x1, Pallas kernels, first_conv(): pl.pallas_call(first_kernel, grid=(8,), out_shape=[jax.ShapeDtypeStruct((...  14.5 us
    pallas_call x1, Pallas kernels, back_active(): pl.pallas_call(active_kernel, grid=(8,), out_shape=[jax.ShapeDtypeStruct(...  11.1 us

profile of v1, /device:TPU:1, one launch (start us, length us, event | category | flops | bytes accessed | tf_op | source)
XLA Modules:
  0.0 260.7 jit_solution(16636486381325952518)
XLA Ops:
  0.6 0.7 pad_bitcast_fusion.4
  1.3 0.7 pad_maximum_fusion.4
  2.0 0.7 broadcast_in_dim.11.tg_ref
  2.6 1.3 pad_convert_fusion.do_ref
  3.9 0.1 copy.64
  4.0 0.7 pad.38.gs_ref
  4.7 1.1 copy.61
  5.7 1.2 copy.65
  7.0 0.8 copy.66
  7.8 0.2 pad_bitcast_fusion.3
  8.1 0.5 pad_maximum_fusion
  8.5 1.8 copy.62
  10.4 1.1 reshape.69
  11.5 1.4 copy.63.w_ref
  12.9 0.9 reshape_reshape.3
  13.7 0.3 reverse_bitcast_fusion
  14.0 1.7 copy.68
  15.7 0.8 copy.82
  16.5 3.5 %copy.80 = bf16[8,32,4,1024]{3,1,0,2:T(8,128)(2,1)} copy(bf16[8,32,4,1024]{3,2,1,0:T(4,128)(2,1)} %param.12) | data formatting | bytes 4194304 | tf_op args[0]
  20.1 29.1 %shard_map.163.h_ref = bf16[2,8,32,1024]{3,2,1,0:T(8,128)(2,1)} custom-call(bf16[4,8,32,1024]{3,2,1,0:T(8,128)(2,1)} %bitcast.58), custom_call_target="tpu_custom_call" | custom-call | tf_op jit(solution)/shard_map/pallas_call | solution.py:156
  49.2 14.5 %shard_map.164 = (f32[8,256,1024]{2,1,0:T(8,128)}, f32[8,256,128]{2,1,0:T(8,128)}) custom-call(bf16[4,8,32,1024]{3,2,1,0:T(8,128)(2,1)} %bitcast.59, bf16[2,8,32,1024]{3,2,1,0:T(8,128)(2,1)} %shard_map.163.h_ref, bf16[256,1728]{1,0:T(8,128)(2,1)} %copy.63.w_ref, bf16[9,1024]{1,0:T(8,128)(2,1)} %constant.15.clone.m_ref), custom_call_target="tpu_custom_call" | custom-call | tf_op jit(solution)/shard_map/pallas_call | solution.py:200
  63.7 9.1 %shard_map.165.st_ref = f32[256,128]{1,0:T(8,128)} custom-call(f32[8,256,128]{2,1,0:T(8,128)} %get-tuple-element.24.st_ref), custom_call_target="tpu_custom_call" | custom-call | tf_op jit(solution)/shard_map/pallas_call | solution.py:245
  72.8 8.8 %shard_map.166.x_ref = bf16[8,128,256]{2,1,0:T(8,128)(2,1)} custom-call(f32[8,256,1024]{2,1,0:T(8,128)} %get-tuple-element.23.x_ref, f32[256,128]{1,0:T(8,128)} %shard_map.165.st_ref, f32[256,128]{1,0:T(8,128)} %pad.38.gs_ref, bf16[256,1024]{1,0:T(8,128)(2,1)} %constant.17.clone.sp_ref), custom_call_target="tpu_custom_call" | custom-call | tf_op jit(solution)/shard_map/pallas_call | solution.py:272
  81.6 9.4 %shard_map.167 = bf16[8,128,256]{2,1,0:T(8,128)(2,1)} custom-call(bf16[8,128,256]{2,1,0:T(8,128)(2,1)} %shard_map.166.x_ref), custom_call_target="tpu_custom_call" | custom-call | tf_op jit(solution)/shard_map/pallas_call | solution.py:114
  91.0 5.6 %shard_map.168 = (f32[16,128,256]{2,1,0:T(8,128)}, bf16[128,512]{1,0:T(8,128)(2,1)}) custom-call(bf16[1024,256]{1,0:T(8,128)(2,1)} %bitcast.62, bf16[128,1728]{1,0:T(8,128)(2,1)} %bitcast.65, bf16[9,256]{1,0:T(8,128)(2,1)} %constant.16.clone.m_ref, bf16[64,256]{1,0:T(8,128)(2,1)} %constant.18.clone.sp_ref), custom_call_target="tpu_custom_call" | custom-call | tf_op jit(solution)/shard_map/pallas_call | solution.py:306
  96.6 20.3 %shard_map.169 = (bf16[8,16,512]{2,1,0:T(8,128)(2,1)}, bf16[8,16,512]{2,1,0:T(8,128)(2,1)}, bf16[8,16,128]{2,1,0:T(8,128)(2,1)}, f32[2,8,128]{2,1,0:T(8,128)}) custom-call(bf16[8,16,512]{2,1,0:T(8,128)(2,1)} %bitcast.78, bf16[16,8,512,128]{3,2,1,0:T(8,128)(2,1)} %bitcast.61, f32[8,128]{1,0:T(8,128)} %pad_convert_fusion.do_ref, f32[8,128]{1,0:T(8,128)} %broadcast_in_dim.11.tg_ref), custom_call_target="tpu_custom_call" | custom-call | tf_op jit(solution)/shard_map/pallas_call | solution.py:384
  117.0 15.6 %shard_map.170 = (bf16[16,64,256]{2,1,0:T(8,128)(2,1)}, f32[128,1728]{1,0:T(8,128)}) custom-call(bf16[1024,256]{1,0:T(8,128)(2,1)} %bitcast.63, f32[16,128,256]{2,1,0:T(8,128)} %get-tuple-element.25.x_ref, bf16[128,512]{1,0:T(8,128)(2,1)} %bitcast.79, bf16[576,384]{1,0:T(8,128)(2,1)} %bitcast.70, bf16[9,256]{1,0:T(8,128)(2,1)} %constant.16.clone.m_ref, ...), custom_call_target="tpu_custom_call" | custom-call | tf_op jit(solution)/shard_map/pallas_call | solution.py:446
  132.6 8.9 %shard_map.171.b_ref = bf16[8,128,256]{2,1,0:T(8,128)(2,1)} custom-call(bf16[8,128,256]{2,1,0:T(8,128)(2,1)} %bitcast.77), custom_call_target="tpu_custom_call" | custom-call | tf_op jit(solution)/shard_map/pallas_call | solution.py:114
  141.6 0.7 reshape.79.fx_ref
  142.4 0.6 slice_reduce_fusion.1
  143.0 0.6 pad.42.bh_ref
  143.6 0.1 copy.69
  143.8 11.1 %shard_map.172 = (bf16[8,256,1024]{2,1,0:T(8,128)(2,1)}, f32[256,128]{1,0:T(8,128)}) custom-call(f32[8,256,1024]{2,1,0:T(8,128)} %get-tuple-element.23.x_ref, bf16[8,128,256]{2,1,0:T(8,128)(2,1)} %shard_map.171.b_ref, f32[256,128]{1,0:T(8,128)} %shard_map.165.st_ref, f32[256,128]{1,0:T(8,128)} %pad.38.gs_ref, bf16[256,1024]{1,0:T(8,128)(2,1)} %constant.17.clone.sp_ref), custom_call_target="tpu_custom_call" | custom-call | tf_op jit(solution)/shard_map/pallas_call | solution.py:481
  154.8 7.6 %shard_map.173 = (f32[256,128]{1,0:T(8,128)}, f32[64,128]{1,0:T(8,128)}) custom-call(f32[256,128]{1,0:T(8,128)} %get-tuple-element.31.s_ref), custom_call_target="tpu_custom_call" | custom-call | tf_op jit(solution)/shard_map/pallas_call | solution.py:514
  162.5 19.5 %shard_map.174 = f32[64,864]{1,0:T(8,128)} custom-call(f32[8,256,1024]{2,1,0:T(8,128)} %get-tuple-element.23.x_ref, bf16[8,256,1024]{2,1,0:T(8,128)(2,1)} %get-tuple-element.30.a_ref, bf16[4,8,32,1024]{3,2,1,0:T(8,128)(2,1)} %bitcast.60, bf16[2,8,32,1024]{3,2,1,0:T(8,128)(2,1)} %shard_map.163.h_ref, f32[256,128]{1,0:T(8,128)} %shard_map.165.st_ref, ...), custom_call_target="tpu_custom_call" | custom-call | tf_op jit(solution)/shard_map/pallas_call | solution.py:560
  182.0 1.1 fusion.4
  183.3 1.2 concatenate.14
  184.5 66.4 %shard_map.175 = (f32[8,16,2176]{2,1,0:T(8,128)}, bf16[16,32,128]{2,1,0:T(8,128)(2,1)}, bf16[16,16,128]{2,1,0:T(8,128)(2,1)}) custom-call(f32[8,16,2176]{2,1,0:T(8,128)} %bitcast.64, bf16[16,32,128]{2,1,0:T(8,128)(2,1)} %reshape.79.fx_ref, bf16[16,128]{1,0:T(8,128)(2,1)} %pad.42.bh_ref), custom_call_target="tpu_custom_call" | custom-call | tf_op jit(solution)/shard_map/pallas_call | solution.py:624
  251.0 1.1 slice_reduce_fusion
  252.1 0.7 reshape_squeeze.6
  252.7 0.9 slice.60
  253.7 0.7 copy.75
  254.3 1.0 reshape.83
  255.3 1.7 fusion
  257.0 1.1 fusion.3
  258.2 0.5 copy.81
  258.7 1.2 copy.74
  259.9 0.8 pad_maximum_fusion.2
  (24 shorter events, 0.3 us)
Async XLA Ops:
  11.5 1.4 copy-start
  116.9 24.6 %copy-start.3 = (bf16[8,16,512]{2,1,0:T(8,128)(2,1)S(1)}, bf16[8,16,512]{2,1,0:T(8,128)(2,1)}, u32[]{:S(2)}) copy-start(bf16[8,16,512]{2,1,0:T(8,128)(2,1)} %get-tuple-element.35) | copy-start | bytes 393220
  116.9 25.4 %copy-start.6 = (f32[2,8,128]{2,1,0:T(8,128)S(1)}, f32[2,8,128]{2,1,0:T(8,128)}, u32[]{:S(2)}) copy-start(f32[2,8,128]{2,1,0:T(8,128)} %get-tuple-element.33) | copy-start | bytes 24580
  117.0 26.0 %copy-start.5 = (bf16[8,16,128]{2,1,0:T(8,128)(2,1)S(1)}, bf16[8,16,128]{2,1,0:T(8,128)(2,1)}, u32[]{:S(2)}) copy-start(bf16[8,16,128]{2,1,0:T(8,128)(2,1)} %get-tuple-element.36) | copy-start | bytes 98308
  162.4 20.7 %copy-start.4 = (f32[64,128]{1,0:T(8,128)S(1)}, f32[64,128]{1,0:T(8,128)}, u32[]{:S(2)}) copy-start(f32[64,128]{1,0:T(8,128)} %get-tuple-element.34) | copy-start | bytes 98308
  182.0 1.3 copy-start.2
  251.0 7.1 %copy-start.1 = (f32[8,16,2176]{2,1,0:T(8,128)S(1)}, f32[8,16,2176]{2,1,0:T(8,128)}, u32[]{:S(2)}) copy-start(f32[8,16,2176]{2,1,0:T(8,128)} %get-tuple-element.37) | copy-start | bytes 3342340

commit v2 on v0

v2 whole, which is shorter than its diff:
```python
import functools

import jax
import jax.numpy as jnp
import numpy as np
from jax import lax
from jax.experimental import pallas as pl
from jax.experimental.pallas import tpu as pltpu
from jax.sharding import PartitionSpec as P

MESH = pl.DeviceIdType.MESH
BF = jnp.bfloat16
F32 = jnp.float32
SPACE, DP = 8, 16
GRID, HALF = 32, 16
EPS = 1e-05
WINDOW = 2
VLIM = 60 << 20

VM = pl.BlockSpec(memory_space=pltpu.VMEM)


def leaky(v):
    return v * (0.65 + 0.35 * jnp.tanh(v))


def slope(v):
    t = jnp.tanh(v)
    return 0.65 + 0.35 * (t + v * (1.0 - t * t))


def shift_masks(extent):
    rows = []
    y, z = np.divmod(np.arange(extent * extent), extent)
    for b in (-1, 0, 1):
        for d in (-1, 0, 1):
            rows.append((y + b >= 0) & (y + b < extent) & (z + d >= 0) & (z + d < extent))
    return np.stack(rows).astype(np.float32)


def spread_matrix(extent):
    y, z = np.divmod(np.arange(extent * extent), extent)
    coarse = (y // 2) * (extent // 2) + z // 2
    return (np.arange((extent // 2) ** 2)[:, None] == coarse[None, :]).astype(np.float32) * 0.125


SHIFTS = [(b, d) for b in (-1, 0, 1) for d in (-1, 0, 1)]


def shifted(block, index, extent, mask):
    b, d = SHIFTS[index]
    step = b * extent + d
    if step == 0:
        return block
    cells = extent * extent
    return pltpu.roll(block, (-step) % cells, 1) * mask[index : index + 1, :]


class Swap:
    def __init__(self, axis, sems, index, source, target):
        self.axis, self.source, self.target = axis, source, target
        self.count = SPACE if axis == "space" else DP
        self.send_sem, self.recv_sem = sems[0].at[index], sems[1].at[index]

    def copy(self, to, source, target, k):
        return pltpu.make_async_remote_copy(
            source, target, self.send_sem.at[k], self.recv_sem.at[k],
            device_id={self.axis: to}, device_id_type=MESH,
        )

    def start_one(self, k):
        me = lax.axis_index(self.axis)
        to = lax.rem(me + k, self.count)
        self.copy(to, self.source(to), self.target(me), k).start()

    def start(self):
        def send(k, carry):
            self.start_one(k)
            return carry

        lax.fori_loop(1, self.count, send, 0)

    def wait_one(self, k):
        fro = lax.rem(lax.axis_index(self.axis) + self.count - k, self.count)
        self.copy(fro, self.source(fro), self.target(fro), k).wait()

    def wait(self):
        def one(k, carry):
            self.wait_one(k)
            return carry

        lax.fori_loop(1, self.count, one, 0)


def greet(axis, count):
    me = lax.axis_index(axis)
    barrier = pltpu.get_barrier_semaphore()

    def signal(k, carry):
        pl.semaphore_signal(
            barrier, inc=1, device_id={axis: lax.rem(me + k, count)}, device_id_type=MESH
        )
        return carry

    lax.fori_loop(1, count, signal, 0)


def nt(a, b):
    return lax.dot_general(a, b, (((1,), (1,)), ((), ())), preferred_element_type=F32)


def nn(a, b):
    return jnp.dot(a, b, preferred_element_type=F32)


def nt_split(a, b):
    high = a.astype(BF)
    low = (a - high.astype(F32)).astype(BF)
    return nt(high, b) + nt(low, b)


def pick(rows, column):
    row = lax.broadcasted_iota(jnp.int32, (rows, 128), 0)
    lane = lax.broadcasted_iota(jnp.int32, (rows, 128), 1)
    return (lane == column(row)).astype(F32).astype(BF)


def two_lanes(first, second):
    lane = lax.broadcasted_iota(jnp.int32, (first.shape[0], 128), 1)
    return jnp.where(lane == 0, first, jnp.where(lane == 1, second, 0.0))


def loop(start, stop, body):
    def step(i, carry):
        body(i)
        return carry

    lax.fori_loop(start, stop, step, 0)


def block_kernel(
    v_ref, cin_ref, wt_ref, gain_ref, bias_ref, out_ref, tg_ref, d_ref, m1_ref, m2_ref, sp1_ref, sp2_ref,
    gout_ref, xout_ref, gdi_ref, pred_ref,
    fall_ref, ball_ref,
    vx, s1, f1, even, wbig, wout, wback, s2, x2, g, gwt, acc, st, gh, gs,
    stile, sgot, fsc, fsend, fx, part, pgot, bfsend, bfgot, bsc, bk,
    own, ogot, fdp, bdp, gsend, ggot, gtile, ggot2, gpiece, ggot3, xsend, xgot, xpiece, xgot2,
    xsum, dv, sp_s, sp_r, dp_s, dp_r, dsem, lsem,
):
    me, group = lax.axis_index("space"), lax.axis_index("dp")
    space, across = (sp_s, sp_r), (dp_s, dp_r)

    greet("space", SPACE)
    greet("dp", DP)
    keep = pltpu.make_async_copy(v_ref.at[me], vx.at[me], lsem)
    keep.start()

    def fetch(d):
        return pltpu.make_async_copy(d_ref.at[d, me], dv.at[d], dsem.at[d])

    for d in range(16):
        fetch(d).start()
    pl.semaphore_wait(pltpu.get_barrier_semaphore(), SPACE - 1 + DP - 1)

    slabs = Swap("space", space, 0, lambda i: v_ref.at[i], lambda i: vx.at[i])
    for k in range(1, WINDOW + 1):
        slabs.start_one(k)

    wbig[...] = jnp.zeros((256, 1728), BF)
    for p in range(4):
        wbig[p * 64 : (p + 1) * 64, p * 288 : p * 288 + 864] = cin_ref[...]
    wout[...] = nt(pick(128, lambda r: r), wt_ref[...]).astype(BF)
    for a in range(3):
        wback[:, a * 128 : (a + 1) * 128] = wt_ref[(2 - a) * 576 : (3 - a) * 576, :]
    same = lax.broadcasted_iota(jnp.int32, (64, 64), 0) == lax.broadcasted_iota(
        jnp.int32, (64, 64), 1
    )
    affine = two_lanes(
        jnp.sum(jnp.where(same, gain_ref[...], 0.0), axis=1, keepdims=True),
        jnp.sum(jnp.where(same, bias_ref[...], 0.0), axis=1, keepdims=True),
    )
    for p in range(4):
        gs[p * 64 : (p + 1) * 64, :] = affine
    s1[0] = jnp.zeros((288, 1024), BF)
    s1[33] = jnp.zeros((288, 1024), BF)
    s2[0] = jnp.zeros((576, 256), BF)
    s2[17] = jnp.zeros((576, 256), BF)
    g[0] = jnp.zeros((128, 256), BF)
    g[17] = jnp.zeros((128, 256), BF)

    def unfold_slab(s):
        masks = m1_ref[...]
        block = vx[s].reshape(128, 1024)
        for i in range(9):
            s1[pl.ds(4 * s + 1, 4), i * 32 : (i + 1) * 32, :] = shifted(
                block, i, GRID, masks
            ).reshape(4, 32, 1024)

    def taps1(s):
        return s1[pl.ds(4 * s, 6)].reshape(1728, 1024)

    def four(rows):
        return rows[0:64] + rows[64:128] + rows[128:192] + rows[192:256]

    def first_slab(s):
        out = nn(wbig[...], taps1(s))
        f1[s] = out
        total = four(jnp.sum(out, axis=1, keepdims=True))
        mean = total * (1.0 / 4096)
        off = out - jnp.concatenate([mean] * 4, axis=0)
        stile[s] = two_lanes(total, four(jnp.sum(off * off, axis=1, keepdims=True)))

    keep.wait()
    unfold_slab(me)

    def arrive(k):
        slabs.wait_one(k)

        @pl.when(k + WINDOW < SPACE)
        def _():
            slabs.start_one(k + WINDOW)

        unfold_slab(lax.rem(me + 8 - k, 8))

    loop(1, 2, arrive)

    def steady(k):
        arrive(k)
        first_slab(lax.rem(me + 9 - k, 8))

    loop(2, 8, steady)
    loop(8, 10, lambda k: first_slab(lax.rem(me + 9 - k, 8)))

    def combine(parts, cells):
        total = functools.reduce(lambda a, b: a + b, parts)
        mean = total[:, 0:1] * (1.0 / (cells * len(parts)))
        moved = 0.0
        for one in parts:
            gap = one[:, 0:1] * (1.0 / cells) - mean
            moved = moved + gap * gap
        return total[:, 0:1], mean, total[:, 1:2] + float(cells) * moved

    total, _, deviation = combine([stile[i] for i in range(8)], 4096)
    own[...] = two_lanes(total, deviation)
    lane = lax.broadcasted_iota(jnp.int32, (1, 128), 1)
    for t in range(4):
        own[0:1, :] += jnp.where(lane == 2 + t, tg_ref[0:1, t : t + 1], 0.0)
    swap = Swap("space", space, 1, lambda i: own, lambda i: sgot.at[i])
    swap.start()
    sgot[me] = own[...]
    swap.wait()
    _, mean, deviation = combine([sgot[i] for i in range(8)], 32768)
    tile = two_lanes(mean, lax.rsqrt(deviation * (1.0 / 262144) + EPS))
    for p in range(4):
        st[p * 64 : (p + 1) * 64, :] = tile

    def whitened(s):
        return (f1[s] - st[:, 0:1]) * st[:, 1:2]

    def normed(white):
        return gs[:, 0:1] * white + gs[:, 1:2]

    def pool_slab(s):
        act = leaky(normed(whitened(s)))
        pairs = jnp.concatenate(
            [act[0:64] + act[64:128], act[128:192] + act[192:256]], axis=0
        )
        pooled = nt_split(pairs, sp1_ref[...]).astype(BF)
        masks = m2_ref[...]
        for i in range(9):
            s2[pl.ds(2 * s + 1, 2), i * 64 : (i + 1) * 64, :] = shifted(
                pooled, i, HALF, masks
            ).reshape(2, 64, 256)

    loop(0, 8, pool_slab)

    def taps2(p):
        return s2[pl.ds(p, 3)].reshape(1728, 256)

    def second_pair(k):
        low = nn(wout[...], taps2(2 * k))
        high = nn(wout[...], taps2(2 * k + 1))
        x2[2 * k] = low
        x2[2 * k + 1] = high
        fsc[k] = nt_split(leaky(low) + leaky(high), sp2_ref[...]).astype(BF)

    loop(0, 8, second_pair)

    feats = jnp.concatenate([fsc[k] for k in range(8)], axis=1)
    fsend[...] = (
        nn(pick(128, lambda r: (r % 16) * 8 + r // 16), feats).astype(BF).reshape(8, 16, 512)
    )
    swap = Swap("space", space, 2, lambda i: fsend.at[i], lambda i: fx.at[i])
    swap.start()
    fx[me] = fsend[me]
    for d in range(16):
        fetch(d).wait()
    swap.wait()
    feats = fx[...].reshape(128, 512)
    row = lax.broadcasted_iota(jnp.int32, (128, 128), 0) % 16
    total = jnp.zeros((128, 128), F32)
    for d in range(16):
        total = total + jnp.where(row == d, nn(feats, dv[d]), 0.0)
    part[...] = jnp.sum(total.reshape(8, 16, 128), axis=1)
    swap = Swap("space", space, 3, lambda i: part, lambda i: pgot.at[i])
    swap.start()
    pgot[me] = part[...]

    spread = nn(pick(256, lambda r: (r % 8) * 16 + r // 16), feats)
    half = lax.broadcasted_iota(jnp.int32, (256, 256), 0) % 16 < 8
    fdp[...] = jnp.where(half, spread[:, :256], spread[:, 256:]).astype(BF).reshape(16, 16, 256)
    swap.wait()

    hidden_pre = jnp.sum(pgot[...], axis=0)
    hidden = leaky(hidden_pre).astype(BF).astype(F32)
    wanted = jnp.concatenate([sgot[i, 0:1, :] for i in range(8)], axis=0)
    mine = lax.broadcasted_iota(jnp.int32, (8, 128), 0) == me
    lane = lax.broadcasted_iota(jnp.int32, (8, 128), 1)
    back = 0.0
    predicted = jnp.zeros((8, 128), F32)
    grad_dense_out = []
    for t in range(4):
        out_t = out_ref[t : t + 1, :].astype(F32)
        prediction = jnp.sum(hidden * out_t, axis=1, keepdims=True)
        misfit = prediction - wanted[:, 2 + t : 3 + t]
        predicted = jnp.where(lane == t, prediction, predicted)
        grad_dense_out.append(
            jnp.sum(jnp.where(mine, hidden * misfit, 0.0), axis=0, keepdims=True)
        )
        back = back + misfit * out_t
    grad_dense_out = jnp.concatenate(grad_dense_out, axis=0)
    pred_ref[...] = jnp.sum(jnp.where(mine, predicted, 0.0), axis=0, keepdims=True)[:, 0:4]
    back = (back * slope(hidden_pre)).astype(BF).astype(F32)
    bdp[...] = jnp.concatenate([back, back], axis=0).astype(BF)
    backs = jnp.broadcast_to(back.reshape(8, 1, 128), (8, 16, 128)).reshape(128, 128).astype(BF)
    row = lax.broadcasted_iota(jnp.int32, (128, 512), 0) % 16
    total = jnp.zeros((128, 512), F32)
    for d in range(16):
        total = jnp.where(row == d, nt(backs, dv[d]), total)
    bfsend[...] = total.reshape(8, 16, 512)
    swap = Swap("space", space, 5, lambda i: bfsend.at[i], lambda i: bfgot.at[i])
    swap.start()
    bfgot[me] = bfsend[me]
    far_feats = Swap("dp", across, 0, lambda i: fdp.at[i], lambda i: fall_ref.at[i])
    far_feats.start()
    fall_ref[group] = fdp[group]
    far_backs = Swap("dp", across, 1, lambda i: bdp, lambda i: ball_ref.at[i])
    far_backs.start()
    ball_ref[group] = bdp[...]
    swap.wait()
    got = bfgot[...].reshape(128, 512)
    high = got.astype(BF)
    low = (got - high.astype(F32)).astype(BF)
    order = pick(128, lambda r: (r % 8) * 16 + r // 8)
    for i, one in enumerate((high, low)):
        ordered = nn(order, one).astype(BF)
        for k in range(8):
            bsc[i, k] = ordered[:, k * 64 : (k + 1) * 64]

    def back_pair(k):
        wide = nn(bsc[0, k], sp2_ref[...]) + nn(bsc[1, k], sp2_ref[...])
        g[2 * k + 1] = (wide * slope(x2[2 * k])).astype(BF)
        g[2 * k + 2] = (wide * slope(x2[2 * k + 1])).astype(BF)

    loop(0, 8, back_pair)
    gwt[...] = jnp.zeros((1728, 128), F32)

    def back_plane(p):
        gwt[...] += nt(taps2(p), g[p + 1])
        taps = nn(wback[...], g[pl.ds(p, 3)].reshape(384, 256))
        masks = m2_ref[...].astype(F32)
        total = taps[256:320]
        for i in range(9):
            if i != 4:
                total = total + shifted(taps[i * 64 : (i + 1) * 64], 8 - i, HALF, masks)
        bk[p] = total.astype(BF)

    loop(0, 16, back_plane)

    gsend[...] = jnp.concatenate(
        [gwt[...].astype(BF), jnp.zeros((320, 128), BF)], axis=0
    ).reshape(8, 256, 128)
    swap1 = Swap("space", space, 6, lambda i: gsend.at[i], lambda i: ggot.at[i])
    swap1.start()
    ggot[me] = gsend[me]

    own[...] = jnp.zeros((64, 128), F32)

    def active_of(s, white):
        wide = nn(bk[pl.ds(2 * s, 2)].reshape(128, 256), sp1_ref[...])
        wide = jnp.concatenate([wide[0:64], wide[0:64], wide[64:128], wide[64:128]], axis=0)
        return wide * slope(normed(white))

    def active_slab(s):
        white = whitened(s)
        active = active_of(s, white)
        own[...] += two_lanes(
            four(jnp.sum(active, axis=1, keepdims=True)),
            four(jnp.sum(active * white, axis=1, keepdims=True)),
        )

    loop(0, 8, active_slab)
    swap = Swap("space", space, 7, lambda i: own, lambda i: ogot.at[i])
    swap.start()
    ogot[me] = own[...]
    swap1.wait()
    gtile[...] = jnp.sum(ggot[...].astype(F32), axis=0).astype(BF).reshape(16, 16, 128)
    swap2 = Swap("dp", across, 2, lambda i: gtile.at[i], lambda i: ggot2.at[i])
    swap2.start()
    ggot2[group] = gtile[group]
    swap.wait()
    tile = jnp.sum(ogot[...], axis=0) * (1.0 / 262144)
    for p in range(4):
        gh[p * 64 : (p + 1) * 64, :] = tile
    acc[...] = jnp.zeros((256, 1728), F32)

    def first_back_slab(s):
        white = whitened(s)
        even[...] = (
            (gs[:, 0:1] * st[:, 1:2])
            * (active_of(s, white) - gh[:, 0:1] - white * gh[:, 1:2])
        ).astype(BF)
        acc[...] += nt(even[...], taps1(s))

    loop(0, 3, first_back_slab)
    far_feats.wait()
    far_backs.wait()
    backs = ball_ref[...].reshape(256, 128)
    upper = lax.broadcasted_iota(jnp.int32, (256, 128), 0) % 16 < 8
    halves = jnp.concatenate(
        [jnp.where(upper, backs, jnp.zeros_like(backs)), jnp.where(upper, jnp.zeros_like(backs), backs)],
        axis=1,
    )
    product = lax.dot_general(
        fall_ref[...].reshape(256, 256), halves, (((0,), (0,)), ((), ())),
        preferred_element_type=F32,
    )
    gdi_ref[0:256, :] = product[:, 0:128]
    gdi_ref[256:512, :] = product[:, 128:256]
    swap2.wait()
    gpiece[...] = jnp.sum(ggot2[...].astype(F32), axis=0).astype(BF)
    swap3 = Swap("dp", across, 3, lambda i: gpiece, lambda i: ggot3.at[i])
    swap3.start()
    ggot3[group] = gpiece[...]
    loop(3, 6, first_back_slab)
    swap3.wait()
    swap4 = Swap("space", space, 8, lambda i: ggot3, lambda i: gout_ref.at[i])
    swap4.start()
    gout_ref[me] = ggot3[...]
    loop(6, 8, first_back_slab)

    grad = functools.reduce(
        lambda a, b: a + b,
        [acc[p * 64 : (p + 1) * 64, p * 288 : p * 288 + 864] for p in range(4)],
    )
    xsend[...] = jnp.zeros((8, 64, 128), F32)
    for t in range(6):
        xsend[t] = grad[:, t * 128 : (t + 1) * 128]
    xsend[6, :, 0:96] = grad[:, 768:864]
    xsend[7] = own[...]
    for i in range(4):
        xsend[6, 4 * i : 4 * i + 4, 96:128] = grad_dense_out[0:4, 32 * i : 32 * i + 32]
    swap = Swap("space", space, 9, lambda i: xsend.at[i], lambda i: xgot.at[i])
    swap.start()
    xgot[me] = xsend[me]
    swap.wait()
    xpiece[...] = jnp.sum(xgot[...], axis=0).astype(BF)
    swap = Swap("dp", across, 4, lambda i: xpiece, lambda i: xgot2.at[i])
    swap.start()
    xgot2[group] = xpiece[...]
    swap.wait()
    xsum[...] = jnp.sum(xgot2[...].astype(F32), axis=0).astype(BF)
    swap = Swap("space", space, 10, lambda i: xsum, lambda i: xout_ref.at[i])
    swap.start()
    xout_ref[me] = xsum[...]
    swap4.wait()
    swap.wait()


def finish_kernel(
    gout_ref, xout_ref, gdi_in_ref, pred_in_ref,
    gci_ref, gnorm_ref, gco_ref, gdi_ref, gdo_ref, pred_ref,
):
    gco_ref[...] = gout_ref[...].reshape(2048, 128)[0:1728].astype(F32)
    gdi_ref[...] = gdi_in_ref[...]
    pred_ref[...] = pred_in_ref[...]
    for t in range(6):
        gci_ref[:, t * 128 : (t + 1) * 128] = xout_ref[t].astype(F32)
    last = xout_ref[6].astype(F32)
    gci_ref[:, 768:864] = last[:, 0:96]
    for i in range(4):
        gdo_ref[:, 32 * i : 32 * i + 32] = last[4 * i : 4 * i + 4, 96:128]
    sums = xout_ref[7].astype(F32).T
    gnorm_ref[...] = jnp.concatenate([sums[1:2, :], sums[0:1, :]], axis=0)


def finish(gout, xout, gdi, pred):
    return pl.pallas_call(
        finish_kernel,
        out_shape=[
            jax.ShapeDtypeStruct(shape, F32)
            for shape in ((64, 864), (2, 64), (1728, 128), (512, 128), (4, 128), (1, 4))
        ],
        in_specs=[VM] * 4,
        out_specs=[VM] * 6,
        compiler_params=pltpu.CompilerParams(vmem_limit_bytes=16 << 20),
    )(gout, xout, gdi, pred)


def block(v, cin, wt, gain, bias, out_t, targets, dense_in, masks1, masks2, spread1, spread2):
    anywhere = pl.BlockSpec(memory_space=pl.ANY)
    scratch = [
        ((16, 16, 256), BF), ((16, 16, 128), BF),
        ((8, 4, 32, 1024), BF), ((34, 288, 1024), BF), ((8, 256, 1024), F32),
        ((256, 1024), BF), ((256, 1728), BF), ((128, 1728), BF), ((576, 384), BF),
        ((18, 576, 256), BF), ((16, 128, 256), F32), ((18, 128, 256), BF),
        ((1728, 128), F32), ((256, 1728), F32), ((256, 128), F32), ((256, 128), F32),
        ((256, 128), F32),
        ((8, 64, 128), F32), ((8, 64, 128), F32), ((8, 128, 64), BF), ((8, 16, 512), BF),
        ((8, 16, 512), BF), ((8, 128), F32), ((8, 8, 128), F32), ((8, 16, 512), F32), ((8, 16, 512), F32), ((2, 8, 128, 64), BF),
        ((16, 64, 256), BF),
        ((64, 128), F32), ((8, 64, 128), F32), ((16, 16, 256), BF), ((16, 128), BF),
        ((8, 256, 128), BF), ((8, 256, 128), BF), ((16, 16, 128), BF), ((16, 16, 128), BF),
        ((16, 128), BF), ((16, 16, 128), BF), ((8, 64, 128), F32), ((8, 64, 128), F32),
        ((64, 128), BF), ((16, 64, 128), BF), ((64, 128), BF), ((16, 512, 128), BF),
    ]
    return pl.pallas_call(
        block_kernel,
        out_shape=[
            jax.ShapeDtypeStruct((8, 16, 16, 128), BF),
            jax.ShapeDtypeStruct((8, 64, 128), BF),
            jax.ShapeDtypeStruct((512, 128), F32),
            jax.ShapeDtypeStruct((1, 4), F32),
        ],
        in_specs=[anywhere] + [VM] * 6 + [anywhere] + [VM] * 4,
        out_specs=[VM] * 4,
        scratch_shapes=[pltpu.VMEM(shape, kind) for shape, kind in scratch]
        + [
            pltpu.SemaphoreType.DMA((11, 8)), pltpu.SemaphoreType.DMA((11, 8)),
            pltpu.SemaphoreType.DMA((5, 16)), pltpu.SemaphoreType.DMA((5, 16)),
            pltpu.SemaphoreType.DMA((16,)), pltpu.SemaphoreType.DMA,
        ],
        compiler_params=pltpu.CompilerParams(
            collective_id=1, has_side_effects=True, vmem_limit_bytes=VLIM
        ),
    )(v, cin, wt, gain, bias, out_t, targets, dense_in, masks1, masks2, spread1, spread2)


def shards(inputs, conv_in, norm_gain, norm_shift, conv_out, dense_in, dense_out, targets):
    masks1 = jnp.asarray(shift_masks(GRID), BF)
    masks2 = jnp.asarray(shift_masks(HALF), BF)
    spread1 = jnp.asarray(spread_matrix(GRID), BF)
    spread2 = jnp.asarray(spread_matrix(HALF), BF)
    v = inputs.transpose(0, 2, 1, 3)
    parts = block(
        v, conv_in, conv_out.T, norm_gain.reshape(1, 64), norm_shift.reshape(1, 64),
        dense_out.T, targets, dense_in.reshape(16, 8, 512, 128),
        masks1, masks2, spread1, spread2,
    )
    grad_in, grad_norm, grad_out, grad_dense, grad_last, predictions = finish(*parts)
    return grad_in, grad_norm, grad_out.T, grad_dense, grad_last.T, predictions


def solution(mesh):
    placed = (P("dp", None, "space", None), P(), P(), P(), P(), P(), P(), P(("dp", "space"), None))
    return jax.shard_map(
        shards,
        mesh=mesh,
        in_specs=placed,
        out_specs=(P(), P(), P(), P(("dp", "space"), None), P(), P(("dp", "space"), None)),
        check_vma=False,
    )
```

time: 1620 us -> 152 us (0.09)
  waiting for transfers between devices: 807 us -> 0 us
  other arithmetic: 267 us -> 0 us
  local copies, waits for them, and re-layouts: 221 us -> 7.2 us
  matrix products: 167 us -> 0 us
  Pallas kernels: 0 us -> 144 us
  blocking collectives: 121 us -> 0 us
    reduce_scatter x1 -> x0, waiting for transfers between devices: 725 us -> none  [shards(): lax.psum_scatter(lax.dot_general(features, back_hidden, (((0,), (0,)), ((...]
    dot_general x23 -> x0, matrix products: 167 us -> none  [the longest x1 78.6 us: shards(): lax.dot_general(back_hidden, dense_in, (((1,), (1,)), ((), ())), preferre...]
    pallas_call x0 -> x2, Pallas kernels: none -> 144 us  [the longest x1 143 us: block(): pl.pallas_call(block_kernel, out_shape=[jax.ShapeDtypeStruct((8, 16, 16,...]
    psum x4 -> x0, blocking collectives: 121 us -> none  [the longest x1 77.2 us: shards(): lax.psum((grad_conv_in, grad_norm_local, grad_conv_out, grad_out_local),...]
    while x416 -> x0, other arithmetic: 107 us -> none
    while x49 -> x0, local copies, waits for them, and re-layouts: 92 us -> none
    psum x1 -> x0, waiting for transfers between devices: 57.1 us -> none  [shards(): lax.psum((grad_conv_in, grad_norm_local, grad_conv_out, grad_out_local),...]
    unnamed x94 -> x9, local copies, waits for them, and re-layouts: 53.9 us -> 7.2 us
  transfers between devices with their start and end apart: 6 -> 0, of which waited for: 5 -> 0; matrix products, arithmetic and copies ran while one was open for 3% -> 0% of each run, Pallas kernels for 0% -> 0%
where the time goes in v2:
time: 152 us
  Pallas kernels  144 us (95%)
  local copies, waits for them, and re-layouts  7.2 us (5%)
    pallas_call x1, Pallas kernels, block(): pl.pallas_call(block_kernel, out_shape=[jax.ShapeDtypeStruct((8, 16, 16,...  143 us
    unnamed x9, local copies, waits for them, and re-layouts  7.2 us

profile of v2, /device:TPU:1, one launch (start us, length us, event | category | flops | bytes accessed | tf_op | source)
XLA Modules:
  0.0 151.6 jit_solution(7133536702496036449)
XLA Ops:
  0.6 3.6 %copy.20 = bf16[8,32,4,1024]{3,1,2,0:T(8,128)(2,1)} copy(bf16[8,32,4,1024]{3,2,1,0:T(4,128)(2,1)} %param.12) | data formatting | bytes 4194304 | tf_op args[0]
  4.3 142.7 %shard_map.163 = (bf16[8,16,16,128]{3,2,1,0:T(8,128)(2,1)}, bf16[8,64,128]{2,1,0:T(8,128)(2,1)}, f32[512,128]{1,0:T(8,128)}, f32[1,4]{1,0:T(1,128)}) custom-call(bf16[8,4,32,1024]{3,2,1,0:T(8,128)(2,1)} %bitcast.11, bf16[64,864]{1,0:T(8,128)(2,1)} %cin_ref.1, bf16[1728,128]{1,0:T(8,128)(2,1)} %bitcast.12, f32[1,64]{1,0:T(1,128)} %bitcast.14, ...), custom_call_target="tpu_custom_call" | custom-call | tf_op jit(solution)/shard_map/pallas_call | solution.py:527
  147.0 0.0 copy-start
  147.0 1.0 copy-done
  148.0 0.0 copy-start.1
  148.0 0.9 copy-done.1
  149.0 0.0 copy-start.2
  149.0 0.9 copy-done.2
  149.9 0.0 copy-start.3
  149.9 0.7 copy-done.3
  150.5 1.1 shard_map.164
Async XLA Ops:
  147.0 1.0 copy-start
  148.0 0.9 copy-start.1
  149.0 0.9 copy-start.2
  149.9 0.7 copy-start.3

commit v3 on v2

--- a/solution.py
+++ b/solution.py
@@ -140,7 +140,7 @@
 
 def block_kernel(
     v_ref, cin_ref, wt_ref, gain_ref, bias_ref, out_ref, tg_ref, d_ref, m1_ref, m2_ref, sp1_ref, sp2_ref,
-    gout_ref, xout_ref, gdi_ref, pred_ref,
+    sums_ref, gdi_ref,
     fall_ref, ball_ref,
     vx, s1, f1, even, wbig, wout, wback, s2, x2, g, gwt, acc, st, gh, gs,
     stile, sgot, fsc, fsend, fx, part, pgot, bfsend, bfgot, bsc, bk,
@@ -329,7 +329,9 @@
         )
         back = back + misfit * out_t
     grad_dense_out = jnp.concatenate(grad_dense_out, axis=0)
-    pred_ref[...] = jnp.sum(jnp.where(mine, predicted, 0.0), axis=0, keepdims=True)[:, 0:4]
+    gdi_ref[512:520, :] = jnp.broadcast_to(
+        jnp.sum(jnp.where(mine, predicted, 0.0), axis=0, keepdims=True), (8, 128)
+    )
     back = (back * slope(hidden_pre)).astype(BF).astype(F32)
     bdp[...] = jnp.concatenate([back, back], axis=0).astype(BF)
     backs = jnp.broadcast_to(back.reshape(8, 1, 128), (8, 16, 128)).reshape(128, 128).astype(BF)
@@ -444,9 +446,9 @@
     ggot3[group] = gpiece[...]
     loop(3, 6, first_back_slab)
     swap3.wait()
-    swap4 = Swap("space", space, 8, lambda i: ggot3, lambda i: gout_ref.at[i])
+    swap4 = Swap("space", space, 8, lambda i: ggot3, lambda i: sums_ref.at[i, pl.ds(0, 16)])
     swap4.start()
-    gout_ref[me] = ggot3[...]
+    sums_ref[me, 0:16] = ggot3[...]
     loop(6, 8, first_back_slab)
 
     grad = functools.reduce(
@@ -469,42 +471,46 @@
     swap.start()
     xgot2[group] = xpiece[...]
     swap.wait()
-    xsum[...] = jnp.sum(xgot2[...].astype(F32), axis=0).astype(BF)
-    swap = Swap("space", space, 10, lambda i: xsum, lambda i: xout_ref.at[i])
-    swap.start()
-    xout_ref[me] = xsum[...]
+    xsum[...] = jnp.sum(xgot2[...].astype(F32), axis=0).astype(BF).reshape(4, 16, 128)
+    swap = Swap("space", space, 10, lambda i: xsum, lambda i: sums_ref.at[i, pl.ds(16, 4)])
+    swap.start()
+    sums_ref[me, 16:20] = xsum[...]
     swap4.wait()
     swap.wait()
 
 
 def finish_kernel(
-    gout_ref, xout_ref, gdi_in_ref, pred_in_ref,
+    sums_ref, dense_ref,
     gci_ref, gnorm_ref, gco_ref, gdi_ref, gdo_ref, pred_ref,
 ):
-    gco_ref[...] = gout_ref[...].reshape(2048, 128)[0:1728].astype(F32)
-    gdi_ref[...] = gdi_in_ref[...]
-    pred_ref[...] = pred_in_ref[...]
+    gco_ref[...] = sums_ref[:, 0:16].reshape(2048, 128)[0:1728].astype(F32)
+    gdi_ref[...] = dense_ref[0:512, :]
+    pred_ref[...] = dense_ref[512:513, 0:4]
+
+    def small(t):
+        return sums_ref[t, 16:20].reshape(64, 128).astype(F32)
+
     for t in range(6):
-        gci_ref[:, t * 128 : (t + 1) * 128] = xout_ref[t].astype(F32)
-    last = xout_ref[6].astype(F32)
+        gci_ref[:, t * 128 : (t + 1) * 128] = small(t)
+    last = small(6)
     gci_ref[:, 768:864] = last[:, 0:96]
     for i in range(4):
         gdo_ref[:, 32 * i : 32 * i + 32] = last[4 * i : 4 * i + 4, 96:128]
-    sums = xout_ref[7].astype(F32).T
+    sums = small(7).T
     gnorm_ref[...] = jnp.concatenate([sums[1:2, :], sums[0:1, :]], axis=0)
 
 
-def finish(gout, xout, gdi, pred):
+def finish(sums, dense_parts):
     return pl.pallas_call(
         finish_kernel,
         out_shape=[
             jax.ShapeDtypeStruct(shape, F32)
             for shape in ((64, 864), (2, 64), (1728, 128), (512, 128), (4, 128), (1, 4))
         ],
-        in_specs=[VM] * 4,
+        in_specs=[VM] * 2,
         out_specs=[VM] * 6,
         compiler_params=pltpu.CompilerParams(vmem_limit_bytes=16 << 20),
-    )(gout, xout, gdi, pred)
+    )(sums, dense_parts)
 
 
 def block(v, cin, wt, gain, bias, out_t, targets, dense_in, masks1, masks2, spread1, spread2):
@@ -522,18 +528,16 @@
         ((64, 128), F32), ((8, 64, 128), F32), ((16, 16, 256), BF), ((16, 128), BF),
         ((8, 256, 128), BF), ((8, 256, 128), BF), ((16, 16, 128), BF), ((16, 16, 128), BF),
         ((16, 128), BF), ((16, 16, 128), BF), ((8, 64, 128), F32), ((8, 64, 128), F32),
-        ((64, 128), BF), ((16, 64, 128), BF), ((64, 128), BF), ((16, 512, 128), BF),
+        ((64, 128), BF), ((16, 64, 128), BF), ((4, 16, 128), BF), ((16, 512, 128), BF),
     ]
     return pl.pallas_call(
         block_kernel,
         out_shape=[
-            jax.ShapeDtypeStruct((8, 16, 16, 128), BF),
-            jax.ShapeDtypeStruct((8, 64, 128), BF),
-            jax.ShapeDtypeStruct((512, 128), F32),
-            jax.ShapeDtypeStruct((1, 4), F32),
+            jax.ShapeDtypeStruct((8, 20, 16, 128), BF),
+            jax.ShapeDtypeStruct((520, 128), F32),
         ],
         in_specs=[anywhere] + [VM] * 6 + [anywhere] + [VM] * 4,
-        out_specs=[VM] * 4,
+        out_specs=[VM] * 2,
         scratch_shapes=[pltpu.VMEM(shape, kind) for shape, kind in scratch]
         + [
             pltpu.SemaphoreType.DMA((11, 8)), pltpu.SemaphoreType.DMA((11, 8)),

time: 152 us -> 150 us (0.987)
  local copies, waits for them, and re-layouts: 7.2 us -> 5.66 us
    unnamed x9 -> x5, local copies, waits for them, and re-layouts: 7.2 us -> 5.66 us
where the time goes in v3:
time: 150 us
  Pallas kernels  144 us (96%)
  local copies, waits for them, and re-layouts  5.66 us (4%)
    pallas_call x1, Pallas kernels, block(): pl.pallas_call(block_kernel, out_shape=[jax.ShapeDtypeStruct((8, 20, 16,...  143 us
    unnamed x5, local copies, waits for them, and re-layouts  5.66 us

profile of v3, /device:TPU:1, one launch (start us, length us, event | category | flops | bytes accessed | tf_op | source)
XLA Modules:
  0.0 150.1 jit_solution(9354007411855276265)
XLA Ops:
  0.6 3.6 %copy.20 = bf16[8,32,4,1024]{3,1,2,0:T(8,128)(2,1)} copy(bf16[8,32,4,1024]{3,2,1,0:T(4,128)(2,1)} %param.12) | data formatting | bytes 4194304 | tf_op args[0]
  4.3 142.7 %shard_map.163 = (bf16[8,20,16,128]{3,2,1,0:T(8,128)(2,1)}, f32[520,128]{1,0:T(8,128)}) custom-call(bf16[8,4,32,1024]{3,2,1,0:T(8,128)(2,1)} %bitcast.11, bf16[64,864]{1,0:T(8,128)(2,1)} %cin_ref.1, bf16[1728,128]{1,0:T(8,128)(2,1)} %bitcast.12, f32[1,64]{1,0:T(1,128)} %bitcast.14, f32[1,64]{1,0:T(1,128)} %bitcast.15, bf16[4,128]{1,0:T(4,128)(2,1)} %bitcast.13, ...), custom_call_target="tpu_custom_call" | custom-call | tf_op jit(solution)/shard_map/pallas_call | solution.py:533
  146.9 0.0 copy-start
  146.9 1.1 copy-done
  148.0 0.0 copy-start.1
  148.0 0.9 copy-done.1
  149.0 1.1 shard_map.164
Async XLA Ops:
  146.9 1.1 copy-start
  148.0 1.0 copy-start.1
